TPU v7x, 32 devices: a whole 2x2x4 slice. The times are simulated.
32 devices in a mesh: seq: 2 (over x), shard: 16 (over z, y, core).
Axes of the slice: x: 2, y: 2, z: 4, core: 2. Of those that a mesh axis runs over, the one named last changes fastest.
Arguments:
- tokens_in: bfloat16 [16, 256, 768], P('shard', 'seq'), may hold values from -6 to 6
- w_query: bfloat16 [768, 768], P(('seq', 'shard')), may hold values from -0.02734375 to 0.02734375
- w_key: bfloat16 [768, 768], P(('seq', 'shard')), may hold values from -0.21875 to 0.21875
- w_value: bfloat16 [768, 768], P(('seq', 'shard')), may hold values from -0.21875 to 0.21875
- output_weight: bfloat16 [768, 768], P(('seq', 'shard')), may hold values from -1.25 to 1.25
- gain_attn: bfloat16 [768], P(('seq', 'shard')), may hold values from 0.25 to 1.75
- gain_moe: bfloat16 [768], P(('seq', 'shard')), may hold values from 0.25 to 1.75
- router_weight: bfloat16 [768, 8], P(('seq', 'shard')), may hold values from -0.16210938 to 0.16210938
- bias_table: bfloat16 [12, 32], P('seq'), may hold values from -4 to 4
- w_expert_in: bfloat16 [16, 768, 1536], P('shard'), may hold values from -0.21875 to 0.21875
- w_expert_out: bfloat16 [16, 1536, 768], P('shard'), may hold values from -0.4375 to 0.4375
- expert_id: int32 [16, 256], P('shard', 'seq'), may hold values from 0 to 7, as said below
- slot_id: int32 [16, 256], P('shard', 'seq'), may hold values from -1 to 19, as said below
- bucket_id: int32 [511], replicated, may hold values from 0 to 31
- cotangent: bfloat16 [16, 256, 768], P('shard', 'seq'), may hold values from -6 to 6
Outputs:
- block_out: bfloat16 [16, 256, 768], P('shard', 'seq')
- grad_tokens: float32 [16, 256, 768], P('shard', 'seq')
- grad_query: float32 [768, 768], P(('seq', 'shard'))
- grad_key: float32 [768, 768], P(('seq', 'shard'))
- grad_value: float32 [768, 768], P(('seq', 'shard'))
- grad_output: float32 [768, 768], P(('seq', 'shard'))
- grad_gain_attn: float32 [768], P(('seq', 'shard'))
- grad_gain_moe: float32 [768], P(('seq', 'shard'))
- grad_router: float32 [768, 8], P(('seq', 'shard'))
- grad_table: float32 [12, 32], P('seq')
- grad_expert_in: float32 [16, 768, 1536], P('shard', None, 'seq')
- grad_expert_out: float32 [16, 1536, 768], P('shard', 'seq')
Inputs may be any that keep to these rules, and one draw needn't show every extreme that they name: `expert_id`: in every aligned block of 128 positions of one sequence some expert is named by more than 20 tokens. `slot_id`: a token's slot is its rank, from 0 in position order, among the tokens of its aligned block of 128 positions that name the same expert; -1 where that rank is 20 or more.
All inputs are finite; a program needn't handle non-finite values.
Results may differ from a plain program's by a relative error of at most 0.014.
Values may be sent and summed in bfloat16 or wider, within the bound.
A program may use at most 128 MiB of HBM per device.

v0:
```python
import jax
import jax.numpy as jnp
from jax import lax
from jax.sharding import PartitionSpec as P

HEAD_DIM = 64


EPS = 1e-06
query_block = 512


def rms_parts(values):
    inverse = lax.rsqrt(jnp.mean(values * values, axis=-1, keepdims=True) + EPS)
    return (values * inverse, inverse)


def rms_back(grad_normed, normed, inverse):
    return inverse * (grad_normed - normed * jnp.mean(grad_normed * normed, axis=-1, keepdims=True))


def spread_offsets(per_offset, block_rows, columns):
    heads_here = per_offset.shape[0]
    period = block_rows + columns
    padded = jnp.pad(per_offset, ((0, 0), (0, 1)))
    tiled = jnp.tile(padded, (1, block_rows))[:, : block_rows * (period - 1)]
    return tiled.reshape(heads_here, block_rows, period - 1)[:, :, block_rows - 1 :]


def offset_sums(grid):
    heads_here, block_rows, columns = grid.shape
    period = block_rows + columns
    widened = jnp.pad(grid, ((0, 0), (0, 0), (block_rows - 1, 0)))
    flat_grid = widened.reshape(heads_here, block_rows * (period - 1))
    flat_grid = jnp.pad(flat_grid, ((0, 0), (0, block_rows)))
    return jnp.sum(flat_grid.reshape(heads_here, block_rows, period), axis=1)[:, : period - 1]


def to_heads(stacked):
    return lax.all_to_all(stacked, "seq", split_axis=2, concat_axis=1, tiled=True)


def to_tokens(stacked):
    return lax.all_to_all(stacked, "seq", split_axis=1, concat_axis=2, tiled=True)


def to_holders(slot_rows, capacity):
    features = slot_rows.shape[1]
    experts = slot_rows.shape[0] // capacity
    outgoing = jnp.broadcast_to(
        slot_rows.reshape(experts, 1, capacity, features), (experts, 2, capacity, features)
    )
    return lax.all_to_all(
        outgoing.reshape(2 * experts, capacity, features),
        "shard",
        split_axis=0,
        concat_axis=0,
        tiled=True,
    )


def to_sources(partial_value, capacity):
    features = partial_value.shape[2]
    returned = lax.all_to_all(partial_value, "shard", split_axis=0, concat_axis=0, tiled=True)
    halves = returned.reshape(-1, 2, capacity, features).astype(jnp.float32)
    return (halves[:, 0] + halves[:, 1]).reshape(-1, features).astype(jnp.bfloat16)


def attend_forward(qkv_heads, per_offset):
    length = qkv_heads.shape[1]
    block_rows = min(length, query_block)
    queries = qkv_heads[0].reshape(length, -1, HEAD_DIM)
    key_heads = qkv_heads[1].reshape(length, -1, HEAD_DIM)
    value_heads = qkv_heads[2].reshape(length, -1, HEAD_DIM)

    def one_block(start):
        scores = jnp.einsum("qhd,khd->hqk", queries, key_heads, preferred_element_type=jnp.float32)
        scores = scores + spread_offsets(per_offset, block_rows, length)
        row_top = jnp.max(scores, axis=-1, keepdims=True)
        weights = jnp.exp(scores - row_top)
        row_total = jnp.sum(weights, axis=-1, keepdims=True)
        probs_low = (weights / row_total).astype(jnp.bfloat16)
        mixed_rows = jnp.einsum(
            "hqk,khd->qhd", probs_low, value_heads, preferred_element_type=jnp.float32
        )
        return (
            mixed_rows.reshape(block_rows, -1).astype(jnp.bfloat16),
            (row_top + jnp.log(row_total))[:, :, 0],
        )

    starts = jnp.arange(length // block_rows, dtype=jnp.int32) * block_rows
    mixed_blocks, log_blocks = lax.map(one_block, starts)
    log_total = jnp.transpose(log_blocks, (1, 0, 2)).reshape(log_blocks.shape[1], length)
    return (mixed_blocks.reshape(length, -1), log_total)


def attend_backward(qkv_heads, per_offset, log_total, grad_mixed):
    length = qkv_heads.shape[1]
    block_rows = min(length, query_block)
    queries = qkv_heads[0].reshape(length, -1, HEAD_DIM)
    key_heads = qkv_heads[1].reshape(length, -1, HEAD_DIM)
    value_heads = qkv_heads[2].reshape(length, -1, HEAD_DIM)
    grad_heads = grad_mixed.reshape(length, -1, HEAD_DIM)
    heads_here = queries.shape[1]

    def one_block(running, start):
        grad_keys, grad_values, grad_offset = running
        scores = jnp.einsum("qhd,khd->hqk", queries, key_heads, preferred_element_type=jnp.float32)
        scores = scores + spread_offsets(per_offset, block_rows, length)
        probs = jnp.exp(scores - log_total[:, :, None])
        grad_probs = jnp.einsum(
            "qhd,khd->hqk", grad_heads, value_heads, preferred_element_type=jnp.float32
        )
        centre = jnp.sum(probs * grad_probs, axis=-1, keepdims=True)
        grad_scores = (probs * (grad_probs - centre)).astype(jnp.bfloat16)
        grad_query_rows = jnp.einsum(
            "hqk,khd->qhd", grad_scores, key_heads, preferred_element_type=jnp.float32
        )
        grad_keys = grad_keys + jnp.einsum(
            "hqk,qhd->khd", grad_scores, queries, preferred_element_type=jnp.float32
        )
        grad_values = grad_values + jnp.einsum(
            "hqk,qhd->khd",
            probs.astype(jnp.bfloat16),
            grad_heads,
            preferred_element_type=jnp.float32,
        )
        pieces = offset_sums(grad_scores.astype(jnp.float32))
        current = grad_offset
        grad_offset = current + pieces
        return (
            (grad_keys, grad_values, grad_offset),
            grad_query_rows.reshape(block_rows, -1).astype(jnp.bfloat16),
        )

    starts = jnp.arange(length // block_rows, dtype=jnp.int32) * block_rows
    initial = (
        jnp.zeros((length, heads_here, HEAD_DIM), jnp.float32),
        jnp.zeros((length, heads_here, HEAD_DIM), jnp.float32),
        jnp.zeros((heads_here, 2 * length - 1), jnp.float32),
    )
    finals, grad_query_blocks = lax.scan(one_block, initial, starts)
    grad_qkv = jnp.stack(
        [
            grad_query_blocks.reshape(length, -1),
            finals[0].reshape(length, -1).astype(jnp.bfloat16),
            finals[1].reshape(length, -1).astype(jnp.bfloat16),
        ]
    )
    return (grad_qkv, finals[2])


def local(
    tokens_in,
    w_query,
    w_key,
    w_value,
    output_weight,
    gain_attn,
    gain_moe,
    router_weight,
    bias_table,
    w_expert_in,
    w_expert_out,
    expert_id,
    slot_id,
    bucket_id,
    cotangent,
):
    tokens_here = tokens_in.shape[1]
    experts = router_weight.shape[1]
    capacity = 2 * max(1, 5 * tokens_here // (8 * experts))
    full_query, full_key, full_value, full_output, full_router, full_gain_attn, full_gain_moe = (
        lax.all_gather(w_query, ("seq", "shard"), axis=0, tiled=True),
        lax.all_gather(w_key, ("seq", "shard"), axis=0, tiled=True),
        lax.all_gather(w_value, ("seq", "shard"), axis=0, tiled=True),
        lax.all_gather(output_weight, ("seq", "shard"), axis=0, tiled=True),
        lax.all_gather(router_weight, ("seq", "shard"), axis=0, tiled=True),
        lax.all_gather(gain_attn, ("seq", "shard"), axis=0, tiled=True),
        lax.all_gather(gain_moe, ("seq", "shard"), axis=0, tiled=True),
    )
    inputs = tokens_in[0].astype(jnp.float32)
    normed_attn, inverse_attn = rms_parts(inputs)
    attention_hidden = (normed_attn * full_gain_attn.astype(jnp.float32)).astype(jnp.bfloat16)
    qkv = jnp.stack(
        [
            jnp.dot(attention_hidden, full_query, preferred_element_type=jnp.float32),
            jnp.dot(attention_hidden, full_key, preferred_element_type=jnp.float32),
            jnp.dot(attention_hidden, full_value, preferred_element_type=jnp.float32),
        ]
    ).astype(jnp.bfloat16)
    qkv_heads = to_heads(qkv)
    buckets = bias_table.shape[1]
    bucket_onehot = (jnp.arange(buckets, dtype=jnp.int32)[:, None] == bucket_id[None, :]).astype(
        jnp.bfloat16
    )
    per_offset = jnp.dot(bias_table, bucket_onehot, preferred_element_type=jnp.float32)
    mixed_heads, log_total = attend_forward(qkv_heads, per_offset)
    mixed_tokens = to_tokens(mixed_heads[None])[0]
    after_attn = inputs + jnp.dot(mixed_tokens, full_output, preferred_element_type=jnp.float32)
    normed_moe, inverse_moe = rms_parts(after_attn)
    mixture_hidden = (normed_moe * full_gain_moe.astype(jnp.float32)).astype(jnp.bfloat16)
    router_logits = jnp.dot(mixture_hidden, full_router, preferred_element_type=jnp.float32)
    row_top = jnp.max(router_logits, axis=-1, keepdims=True)
    gate_weights = jnp.exp(router_logits - row_top)
    gate_probs = gate_weights / jnp.sum(gate_weights, axis=-1, keepdims=True)
    chosen = (expert_id[0][:, None] == jnp.arange(experts, dtype=jnp.int32)[None, :]).astype(
        jnp.float32
    )
    picked = jnp.sum(gate_probs * chosen, axis=-1, keepdims=True)
    slot_of = jnp.where(slot_id[0] >= 0, expert_id[0] * capacity + slot_id[0], -1)
    dispatch = (
        slot_of[:, None] == jnp.arange(experts * capacity, dtype=jnp.int32)[None, :]
    ).astype(jnp.bfloat16)
    buffer = jnp.einsum(
        "ts,td->sd", dispatch, mixture_hidden, preferred_element_type=jnp.float32
    ).astype(jnp.bfloat16)
    received = to_holders(buffer, capacity)
    inner_weight = w_expert_in[0]
    outer_weight = w_expert_out[0]
    pre_act = jnp.einsum("nsd,df->nsf", received, inner_weight, preferred_element_type=jnp.float32)
    activated = jax.nn.gelu(pre_act).astype(jnp.bfloat16)
    partial_terms = jnp.einsum(
        "nsf,fd->nsd", activated, outer_weight, preferred_element_type=jnp.float32
    )
    partial_value = partial_terms.astype(jnp.bfloat16)
    expert_slots = to_sources(partial_value, capacity)
    combined = jnp.dot(dispatch, expert_slots, preferred_element_type=jnp.float32)
    block_out = after_attn + picked * combined
    grad_out = cotangent[0].astype(jnp.float32)
    grad_picked = jnp.sum(grad_out * combined, axis=-1, keepdims=True)
    scaled = (picked * grad_out).astype(jnp.bfloat16)
    grad_slots = jnp.einsum(
        "ts,td->sd", dispatch, scaled, preferred_element_type=jnp.float32
    ).astype(jnp.bfloat16)
    grad_received = to_holders(grad_slots, capacity)
    grad_activated = jnp.einsum(
        "nsd,fd->nsf", grad_received, outer_weight, preferred_element_type=jnp.float32
    )
    gelu_value, gelu_pull = jax.vjp(jax.nn.gelu, pre_act)
    grad_pre = gelu_pull(grad_activated)[0].astype(jnp.bfloat16)
    grad_expert_out = jnp.einsum(
        "nsf,nsd->fd", activated, grad_received, preferred_element_type=jnp.float32
    )
    grad_expert_in = jnp.einsum(
        "nsd,nsf->df", received, grad_pre, preferred_element_type=jnp.float32
    )
    half_terms = jnp.einsum(
        "nsf,df->nsd", grad_pre, inner_weight, preferred_element_type=jnp.float32
    )
    grad_half = half_terms.astype(jnp.bfloat16)
    grad_buffer = to_sources(grad_half, capacity)
    grad_gates = chosen * grad_picked
    grad_logits = gate_probs * (
        grad_gates - jnp.sum(gate_probs * grad_gates, axis=-1, keepdims=True)
    )
    grad_logits = grad_logits.astype(jnp.bfloat16)
    grad_router = jnp.einsum(
        "td,te->de", mixture_hidden, grad_logits, preferred_element_type=jnp.float32
    )
    grad_hidden_moe = jnp.einsum(
        "te,de->td", grad_logits, full_router, preferred_element_type=jnp.float32
    )
    grad_hidden_moe = grad_hidden_moe + jnp.dot(
        dispatch, grad_buffer, preferred_element_type=jnp.float32
    )
    grad_gain_moe = jnp.sum(grad_hidden_moe * normed_moe, axis=0)
    grad_mid = grad_out + rms_back(
        grad_hidden_moe * full_gain_moe.astype(jnp.float32), normed_moe, inverse_moe
    )
    grad_branch = grad_mid.astype(jnp.bfloat16)
    grad_output = jnp.einsum(
        "td,te->de", mixed_tokens, grad_branch, preferred_element_type=jnp.float32
    )
    grad_mixed = jnp.einsum(
        "te,de->td", grad_branch, full_output, preferred_element_type=jnp.float32
    ).astype(jnp.bfloat16)
    grad_mixed_heads = to_heads(grad_mixed[None])[0]
    grad_qkv_heads, grad_offset = attend_backward(
        qkv_heads, per_offset, log_total, grad_mixed_heads
    )
    grad_table = jnp.einsum(
        "ho,bo->hb", grad_offset, bucket_onehot.astype(jnp.float32), precision=lax.Precision.HIGHEST
    )
    grad_table = lax.psum(grad_table, "shard")
    grad_qkv = to_tokens(grad_qkv_heads)
    grad_hidden_attn = jnp.einsum(
        "te,de->td", grad_qkv[0], full_query, preferred_element_type=jnp.float32
    )
    grad_hidden_attn = grad_hidden_attn + jnp.einsum(
        "te,de->td", grad_qkv[1], full_key, preferred_element_type=jnp.float32
    )
    grad_hidden_attn = grad_hidden_attn + jnp.einsum(
        "te,de->td", grad_qkv[2], full_value, preferred_element_type=jnp.float32
    )
    grad_gain_attn = jnp.sum(grad_hidden_attn * normed_attn, axis=0)
    grad_tokens = grad_mid + rms_back(
        grad_hidden_attn * full_gain_attn.astype(jnp.float32), normed_attn, inverse_attn
    )
    qkv_share = lax.psum_scatter(
        jnp.einsum("tr,ktd->rkd", attention_hidden, grad_qkv, preferred_element_type=jnp.float32),
        ("seq", "shard"),
        scatter_dimension=0,
        tiled=True,
    )
    output_share, router_share, gain_attn_share, gain_moe_share = (
        lax.psum_scatter(grad_output, ("seq", "shard"), scatter_dimension=0, tiled=True),
        lax.psum_scatter(grad_router, ("seq", "shard"), scatter_dimension=0, tiled=True),
        lax.psum_scatter(grad_gain_attn, ("seq", "shard"), scatter_dimension=0, tiled=True),
        lax.psum_scatter(grad_gain_moe, ("seq", "shard"), scatter_dimension=0, tiled=True),
    )
    expert_in_share, expert_out_share = (
        lax.psum_scatter(
            grad_expert_in[None].astype(jnp.bfloat16), "seq", scatter_dimension=2, tiled=True
        ).astype(jnp.float32),
        lax.psum_scatter(
            grad_expert_out[None].astype(jnp.bfloat16), "seq", scatter_dimension=1, tiled=True
        ).astype(jnp.float32),
    )
    return (
        block_out.astype(jnp.bfloat16)[None],
        grad_tokens[None],
        qkv_share[:, 0],
        qkv_share[:, 1],
        qkv_share[:, 2],
        output_share,
        gain_attn_share,
        gain_moe_share,
        router_share,
        grad_table,
        expert_in_share,
        expert_out_share,
    )


def solution(mesh):
    return jax.shard_map(
        local,
        mesh=mesh,
        in_specs=(
            P("shard", "seq", None),
            P(("seq", "shard"), None),
            P(("seq", "shard"), None),
            P(("seq", "shard"), None),
            P(("seq", "shard"), None),
            P(("seq", "shard")),
            P(("seq", "shard")),
            P(("seq", "shard"), None),
            P("seq", None),
            P("shard", None, None),
            P("shard", None, None),
            P("shard", "seq"),
            P("shard", "seq"),
            P(),
            P("shard", "seq", None),
        ),
        out_specs=(
            P("shard", "seq", None),
            P("shard", "seq", None),
            P(("seq", "shard"), None),
            P(("seq", "shard"), None),
            P(("seq", "shard"), None),
            P(("seq", "shard"), None),
            P(("seq", "shard")),
            P(("seq", "shard")),
            P(("seq", "shard"), None),
            P("seq", None),
            P("shard", None, "seq"),
            P("shard", "seq", None),
        ),
        check_vma=False,
    )
```

profile of v0, /device:TPU:0, one launch (start us, length us, event | category | flops | bytes accessed | tf_op | source)
XLA Modules:
  0.0 677.1 jit_solution(17858655014230681278)
XLA Ops:
  13.6 42.1 %all-reduce.9 = (bf16[768]{0:T(1024)(128)(2,1)S(1)}, bf16[768]{0:T(1024)(128)(2,1)S(1)}) all-reduce(bf16[768]{0:T(1024)(128)(2,1)S(1)} %dynamic-update-slice, bf16[768]{0:T(1024)(128)(2,1)S(1)} %dynamic-update-slice.1), channel_id=1, replica_groups=mesh['seq'=2,'shard'=16] {'seq','shard'}, use_global_device_ids=true, to_apply=%add.3 | all-reduce | flops 1536 | bytes 6144
  56.3 11.6 %all-gather.10.cloned.1.call-done = bf16[768,768]{1,0:T(8,128)(2,1)} async-done(((bf16[24,768]{1,0:T(8,128)(2,1)}), bf16[768,768]{1,0:T(8,128)(2,1)}) %all-gather.10.cloned.1.call-update) | async-done | bytes 1179664 | tf_op jit(solution)/shard_map/all_gather | solution.py:176
  69.6 54.2 %all-gather.8.cloned.1.call-done = bf16[768,768]{1,0:T(8,128)(2,1)} async-done(((bf16[24,768]{1,0:T(8,128)(2,1)}), bf16[768,768]{1,0:T(8,128)(2,1)}) %all-gather.8.cloned.1.call-update) | async-done | bytes 1179664 | tf_op jit(solution)/shard_map/all_gather | solution.py:175
  125.5 54.2 %all-gather.6.cloned.1.call-done = bf16[768,768]{1,0:T(8,128)(2,1)} async-done(((bf16[24,768]{1,0:T(8,128)(2,1)}), bf16[768,768]{1,0:T(8,128)(2,1)}) %all-gather.6.cloned.1.call-update) | async-done | bytes 1179664 | tf_op jit(solution)/shard_map/all_gather | solution.py:174
  182.7 4.1 all-to-all-start
  191.3 6.4 reshape.218
  197.7 3.3 slice.84
  201.0 3.0 copy.127
  212.2 3.4 all-to-all-start.1
  215.7 5.1 all-to-all-done.1
  221.2 14.4 %all-gather.12.cloned.1.call-done = bf16[768,768]{1,0:T(8,128)(2,1)} async-done(((bf16[24,768]{1,0:T(8,128)(2,1)}), bf16[768,768]{1,0:T(8,128)(2,1)}) %all-gather.12.cloned.1.call-update) | async-done | bytes 1179664 | tf_op jit(solution)/shard_map/all_gather | solution.py:177
  241.2 21.7 %all_to_all.83 = bf16[16,20,768]{2,1,0:T(8,128)(2,1)S(1)} all-to-all(bf16[16,20,768]{2,1,0:T(8,128)(2,1)S(1)} %bitcast.239), channel_id=1, replica_groups=mesh['seq'=2,'shard'=16] {'shard'}, dimensions={0} | all-to-all | bytes 983040 | tf_op jit(solution)/shard_map/all_to_all | solution.py:53
  270.5 4.3 all-to-all-start.3
  274.8 45.1 %all-gather = bf16[32,24,8]{1,2,0:T(8,128)(2,1)S(1)} all-gather(bf16[1,24,8]{1,2,0:T(8,128)(2,1)S(1)} %bitcast.263), channel_id=1, replica_groups=mesh['seq'=2,'shard'=16] {'seq','shard'}, dimensions={0}, use_global_device_ids=true | all-gather | bytes 12672 | tf_op jit(solution)/shard_map/all_gather | solution.py:178
  331.2 19.8 %all_to_all.84 = bf16[16,20,768]{2,1,0:T(8,128)(2,1)S(1)} all-to-all(bf16[16,20,768]{2,1,0:T(8,128)(2,1)S(1)} %bitcast.240), channel_id=1, replica_groups=mesh['seq'=2,'shard'=16] {'shard'}, dimensions={0} | all-to-all | bytes 983040 | tf_op jit(solution)/shard_map/all_to_all | solution.py:53
  351.1 4.1 fusion.8
  360.1 4.8 fusion.1
  366.2 3.7 fusion.20
  369.8 3.8 all-to-all-start.5
  374.0 15.2 %all-to-all-done.5 = bf16[16,20,768]{2,1,0:T(8,128)(2,1)S(1)} async-done(((bf16[16,20,768]{2,1,0:T(8,128)(2,1)}), bf16[16,20,768]{2,1,0:T(8,128)(2,1)S(1)}, u32[]{:S(2)}, u32[]{:S(2)}) %all-to-all-start.5) | async-done | bytes 491552 | tf_op jit(solution)/shard_map/all_to_all | solution.py:64
  399.3 3.4 all-to-all-start.6
  403.6 6.8 %all-to-all-done.6 = bf16[2,2,24576]{2,1,0:T(2,128)(2,1)S(1)} async-done(((bf16[2,2,24576]{2,1,0:T(2,128)(2,1)}), bf16[2,2,24576]{2,1,0:T(2,128)(2,1)S(1)}, u32[]{:S(2)}, u32[]{:S(2)}) %all-to-all-start.6) | async-done | bytes 196640 | tf_op jit(solution)/shard_map/all_to_all | solution.py:40
  416.8 21.0 %all_to_all.85 = bf16[3,256,384]{2,0,1:T(4,128)(2,1)S(1)} all-to-all(bf16[3,256,384]{2,0,1:T(4,128)(2,1)S(1)} %pad_maximum_fusion), channel_id=1, replica_groups=mesh['seq'=2,'shard'=16] {'seq'}, dimensions={1} | all-to-all | bytes 1179648 | tf_op jit(solution)/shard_map/all_to_all | solution.py:44
  438.8 4.1 fusion.58
  447.2 3.9 reshape.244
  451.1 3.1 reshape.221
  456.4 33.3 %psum.7 = f32[6,32]{1,0:T(8,128)} all-reduce(f32[6,32]{1,0:T(8,128)S(1)} %fusion.72), channel_id=1, replica_groups=mesh['seq'=2,'shard'=16] {'shard'}, use_global_device_ids=true, to_apply=%region_20.21 | all-reduce | flops 192 | bytes 1536 | tf_op jit(solution)/shard_map/psum | solution.py:285
  493.4 38.6 %all-reduce.8 = (f32[768]{0:T(1024)S(1)}, f32[768]{0:T(1024)S(1)}, f32[768,8]{0,1:T(8,128)S(1)}) all-reduce(f32[768]{0:T(1024)S(1)} %get-tuple-element.57, f32[768]{0:T(1024)S(1)} %get-tuple-element.55, f32[768,8]{0,1:T(8,128)S(1)} %copy-done.26), channel_id=4, replica_groups=mesh['seq'=2,'shard'=16] {'seq','shard'}, use_global_device_ids=true, to_apply=%region_15.16.clone | all-reduce | flops 7680 | bytes 61440
  534.8 3.0 convert_element_type.250
  537.8 2.8 convert_element_type.253
  540.6 24.2 %reduce-scatter.6.cloned.1.call-done = f32[24,3,768]{2,0,1:T(8,128)} async-done(((f32[768,3,768]{2,0,1:T(8,128)}), f32[24,3,768]{2,0,1:T(8,128)}) %reduce-scatter.6.cloned.1.call-update) | async-done | bytes 221200 | tf_op jit(solution)/shard_map/reduce_scatter | solution.py:300
  566.5 103.5 %reduce-scatter.8.cloned.1.call-done = f32[24,768]{1,0:T(8,128)} async-done(((f32[768,768]{1,0:T(8,128)}), f32[24,768]{1,0:T(8,128)}) %reduce-scatter.8.cloned.1.call-update) | async-done | bytes 73744 | tf_op jit(solution)/shard_map/reduce_scatter | solution.py:307
  (244 shorter events, 89.6 us)
Async XLA Ops:
  7.2 260.8 %copy-start = (bf16[1,1536,768]{2,1,0:T(8,128)(2,1)S(1)}, bf16[1,1536,768]{2,1,0:T(8,128)(2,1)}, u32[]{:S(2)}) copy-start(bf16[1,1536,768]{2,1,0:T(8,128)(2,1)} %param.25) | copy-start | bytes 7077892
  7.2 172.5 %copy-start.4 = (bf16[1,128,768]{2,1,0:T(8,128)(2,1)S(1)}, bf16[1,128,768]{2,1,0:T(8,128)(2,1)}, u32[]{:S(2)}) copy-start(bf16[1,128,768]{2,1,0:T(8,128)(2,1)} %param.15) | copy-start | bytes 589828
  7.2 60.6 %all-gather.10.cloned.1.call-start = ((), (), s32[]{:S(2)}) async-start(), calls=%async_computation.14 | async-start | bytes 1216512 | tf_op jit(solution)/shard_map/all_gather | solution.py:176
  7.9 115.8 %all-gather.8.cloned.1.call-start = ((), (), s32[]{:S(2)}) async-start(), calls=%async_computation.13 | async-start | bytes 1216512 | tf_op jit(solution)/shard_map/all_gather | solution.py:175
  8.7 171.0 %all-gather.6.cloned.1.call-start = ((), (), s32[]{:S(2)}) async-start(), calls=%async_computation.12 | async-start | bytes 1216512 | tf_op jit(solution)/shard_map/all_gather | solution.py:174
  9.4 226.2 %all-gather.12.cloned.1.call-start = ((), (), s32[]{:S(2)}) async-start(), calls=%async_computation.15 | async-start | bytes 1216512 | tf_op jit(solution)/shard_map/all_gather | solution.py:177
  11.9 167.8 %copy-start.32 = (f32[128]{0:T(128)}, f32[128]{0:T(128)S(1)}, u32[]{:S(2)}) copy-start(f32[128]{0:T(128)S(1)} %add_rsqrt_fusion.1) | copy-start | bytes 1540
  182.7 21.3 %all-to-all-start = ((bf16[3,128,768]{1,0,2:T(4,128)(2,1)}), bf16[3,128,768]{1,0,2:T(4,128)(2,1)S(1)}, u32[]{:S(2)}, u32[]{:S(2)}) async-start(bf16[3,128,768]{1,0,2:T(4,128)(2,1)} %copy.95), calls=%async_computation | async-start | bytes 1572864 | tf_op jit(solution)/shard_map/all_to_all | solution.py:40
  207.7 7.9 %copy-start.47 = (s32[1,128]{1,0:T(1,128)S(1)}, s32[1,128]{1,0:T(1,128)}, u32[]{:S(2)}) copy-start(s32[1,128]{1,0:T(1,128)} %param.26) | copy-start | bytes 1540
  207.8 7.9 %copy-start.57 = (s32[1,128]{1,0:T(1,128)S(1)}, s32[1,128]{1,0:T(1,128)}, u32[]{:S(2)}) copy-start(s32[1,128]{1,0:T(1,128)} %param.27) | copy-start | bytes 1540
  212.2 8.6 %all-to-all-start.1 = ((bf16[2,2,24576]{2,1,0:T(2,128)(2,1)}), bf16[2,2,24576]{2,1,0:T(2,128)(2,1)S(1)}, u32[]{:S(2)}, u32[]{:S(2)}) async-start(bf16[2,2,24576]{2,1,0:T(2,128)(2,1)} %reshape.246), calls=%async_computation.1 | async-start | bytes 393216 | tf_op jit(solution)/shard_map/all_to_all | solution.py:44
  215.6 24.6 %copy-start.45 = (s32[128]{0:T(128)}, s32[128]{0:T(128)S(1)}, u32[]{:S(2)}) copy-start(s32[128]{0:T(128)S(1)} %compare_select_fusion) | copy-start | bytes 1540
  215.7 24.6 %copy-start.28 = (f32[768]{0:T(1024)}, f32[768]{0:T(1024)S(1)}, u32[]{:S(2)}) copy-start(f32[768]{0:T(1024)S(1)} %convert_element_type.211) | copy-start | bytes 9220
  221.2 16.2 %copy-start.10 = (bf16[1,128,2,384]{1,3,2,0:T(8,128)(2,1)}, bf16[1,128,2,384]{1,3,2,0:T(8,128)(2,1)S(1)}, u32[]{:S(2)}) copy-start(bf16[1,128,2,384]{1,3,2,0:T(8,128)(2,1)S(1)} %copy.100) | copy-start | bytes 589828
  237.4 29.2 %copy-start.55 = (f32[128]{0:T(128)}, f32[128]{0:T(128)S(1)}, u32[]{:S(2)}) copy-start(f32[128]{0:T(128)S(1)} %add_rsqrt_fusion) | copy-start | bytes 1540
  237.5 84.1 %copy-start.8 = (bf16[128,768]{1,0:T(8,128)(2,1)}, bf16[128,768]{1,0:T(8,128)(2,1)S(1)}, u32[]{:S(2)}) copy-start(bf16[128,768]{1,0:T(8,128)(2,1)S(1)} %multiply_convert_fusion.2) | copy-start | bytes 589828
  270.5 51.9 %all-to-all-start.3 = ((bf16[16,20,768]{2,1,0:T(8,128)(2,1)}), bf16[16,20,768]{2,1,0:T(8,128)(2,1)}, u32[]{:S(2)}, u32[]{:S(2)}) async-start(bf16[16,20,768]{2,1,0:T(8,128)(2,1)} %fusion.23), calls=%async_computation.3 | async-start | bytes 1179648 | tf_op jit(solution)/shard_map/all_to_all | solution.py:64
  274.8 51.3 %copy-start.14 = (bf16[1,128,768]{2,1,0:T(8,128)(2,1)S(1)}, bf16[1,128,768]{2,1,0:T(8,128)(2,1)}, u32[]{:S(2)}) copy-start(bf16[1,128,768]{2,1,0:T(8,128)(2,1)} %param.29) | copy-start | bytes 589828
  274.8 260.0 %reduce-scatter.10.cloned.1.call-start = ((), (), s32[]{:S(2)}) async-start(), calls=%async_computation.18 | async-start | bytes 3538944 | tf_op jit(solution)/shard_map/reduce_scatter | solution.py:313
  359.0 178.7 %reduce-scatter.12.cloned.1.call-start = ((), (), s32[]{:S(2)}) async-start(), calls=%async_computation.19 | async-start | bytes 3538944 | tf_op jit(solution)/shard_map/reduce_scatter | solution.py:316
  366.1 7.5 %copy-start.42 = (f32[128]{0:T(128)S(1)}, f32[128]{0:T(128)}, u32[]{:S(2)}) copy-start(f32[128]{0:T(128)} %copy-done.41) | copy-start | bytes 1540
  366.1 7.5 %copy-start.49 = (s32[1,128]{1,0:T(1,128)S(1)}, s32[1,128]{1,0:T(1,128)}, u32[]{:S(2)}) copy-start(s32[1,128]{1,0:T(1,128)} %param.26) | copy-start | bytes 1540
  366.2 7.5 %copy-start.51 = (f32[128]{0:T(128)S(1)}, f32[128]{0:T(128)}, u32[]{:S(2)}) copy-start(f32[128]{0:T(128)} %get-tuple-element.59) | copy-start | bytes 1540
  369.8 19.3 %all-to-all-start.5 = ((bf16[16,20,768]{2,1,0:T(8,128)(2,1)}), bf16[16,20,768]{2,1,0:T(8,128)(2,1)S(1)}, u32[]{:S(2)}, u32[]{:S(2)}) async-start(bf16[16,20,768]{2,1,0:T(8,128)(2,1)} %fusion.20), calls=%async_computation.5 | async-start | bytes 1179648 | tf_op jit(solution)/shard_map/all_to_all | solution.py:64
  395.4 15.6 %copy-start.3 = (f32[6,256,256]{1,2,0:T(8,128)S(1)}, f32[6,256,256]{1,2,0:T(8,128)}, u32[]{:S(2)}) copy-start(f32[6,256,256]{1,2,0:T(8,128)} %copy-done.2) | copy-start | bytes 4718596
  399.3 11.1 %all-to-all-start.6 = ((bf16[2,2,24576]{2,1,0:T(2,128)(2,1)}), bf16[2,2,24576]{2,1,0:T(2,128)(2,1)S(1)}, u32[]{:S(2)}, u32[]{:S(2)}) async-start(bf16[2,2,24576]{2,1,0:T(2,128)(2,1)} %reshape.248), calls=%async_computation.6 | async-start | bytes 393216 | tf_op jit(solution)/shard_map/all_to_all | solution.py:40
  402.8 9.7 %copy-start.17 = (bf16[256,6,64]{0,2,1:T(8,128)(2,1)S(1)}, bf16[256,6,64]{0,2,1:T(8,128)(2,1)}, u32[]{:S(2)}) copy-start(bf16[256,6,64]{0,2,1:T(8,128)(2,1)} %copy-done.16) | copy-start | bytes 589828
  402.8 162.1 %reduce-scatter.6.cloned.1.call-start = ((), (), s32[]{:S(2)}) async-start(), calls=%async_computation.16 | async-start | bytes 7299072 | tf_op jit(solution)/shard_map/reduce_scatter | solution.py:300
  416.8 22.1 %copy-start.33 = (f32[128]{0:T(128)S(1)}, f32[128]{0:T(128)}, u32[]{:S(2)}) copy-start(f32[128]{0:T(128)} %copy-done.32) | copy-start | bytes 1540
  443.0 227.0 %reduce-scatter.8.cloned.1.call-start = ((), (), s32[]{:S(2)}) async-start(), calls=%async_computation.17 | async-start | bytes 2433024 | tf_op jit(solution)/shard_map/reduce_scatter | solution.py:307
  456.3 35.9 %copy-start.6 = (bf16[768,768]{1,0:T(8,128)(2,1)S(1)}, bf16[768,768]{1,0:T(8,128)(2,1)}, u32[]{:S(2)}) copy-start(bf16[768,768]{1,0:T(8,128)(2,1)} %all-gather.8.cloned.1.call-done) | copy-start | bytes 3538948
  534.8 135.2 %copy-start.1 = (bf16[1,1536,768]{2,1,0:T(8,128)(2,1)S(1)}, bf16[1,1536,768]{2,1,0:T(8,128)(2,1)}, u32[]{:S(2)}) copy-start(bf16[1,1536,768]{2,1,0:T(8,128)(2,1)} %param.25) | copy-start | bytes 7077892
  (42 other events, 115.0 us)
Sparse Core Ops, SparseCore 0:
  10.9 56.8 all-gather.9
  70.7 53.0 all-gather.7
  126.7 52.9 all-gather.5
  182.5 53.1 all-gather.11
  359.2 32.5 reduce-scatter.9
  393.9 44.5 reduce-scatter.11
  444.2 120.6 reduce-scatter.5
  571.5 98.3 reduce-scatter.7
where the time goes:
time: 682 us; the launch traced here: 677 us
  waiting for transfers between devices  292 us (43%)
  blocking collectives  222 us (33%)
  local copies, waits for them, and re-layouts  58.3 us (9%)
  matrix products  48.6 us (7%)
  other arithmetic  21.8 us (3%)
  starting transfers between devices  19.5 us (3%)
  between operations  15.5 us (2%)
    reduce_scatter x1, waiting for transfers between devices, local(): lax.psum_scatter(grad_output, ('seq', 'shard'), scatter_dimension=0, tile...  103 us
    unnamed x2, blocking collectives  80.7 us
    all_gather x1, waiting for transfers between devices, local(): lax.all_gather(w_key, ('seq', 'shard'), axis=0, tiled=True)  54.2 us
    all_gather x1, waiting for transfers between devices, local(): lax.all_gather(w_query, ('seq', 'shard'), axis=0, tiled=True)  54.2 us
    all_gather x1, blocking collectives, local(): lax.all_gather(router_weight, ('seq', 'shard'), axis=0, tiled=True)  45.1 us
    all_to_all x2, blocking collectives, to_holders(): lax.all_to_all(outgoing.reshape(2 * experts, capacity, features), 'shard'...  41.6 us
    psum x1, blocking collectives, local(): grad_table = lax.psum(grad_table, 'shard')  33.3 us
    unnamed x145, local copies, waits for them, and re-layouts  24.8 us
  transfers between devices with their start and end apart: 13, of which 9 were waited for; matrix products, arithmetic and copies ran while one was open for 14% of the time, Pallas kernels for 0%

commit v1 on v0

v1 whole, which is shorter than its diff:
```python
import functools

import jax
import jax.numpy as jnp
from jax import lax
from jax.experimental import pallas as pl
from jax.experimental.pallas import tpu as pltpu
from jax.sharding import PartitionSpec as P

HEAD_DIM = 64
EPS = 1e-06
MESH = pl.DeviceIdType.MESH
VMEM_LIMIT = 56 * 1024 * 1024
BF16 = jnp.bfloat16
F32 = jnp.float32


def round_up(value, step):
    return (value + step - 1) // step * step


def coordinates(bits):
    shard = lax.axis_index("shard")
    return [lax.axis_index("seq")] + [(shard // 2**b) % 2 for b in reversed(range(bits))]


def partner(dim, bits):
    seq, shard = lax.axis_index("seq"), lax.axis_index("shard")
    if dim == 0:
        return (1 - seq, shard)
    step = 2 ** (bits - dim)
    return (seq, shard + (1 - 2 * ((shard // step) % 2)) * step)


def greet(targets):
    barrier = pltpu.get_barrier_semaphore()
    for target in targets:
        pl.semaphore_signal(barrier, inc=1, device_id=target, device_id_type=MESH)
    pl.semaphore_wait(barrier, len(targets))


def gather_orders(bits):
    far = list(range(1, bits - 1))
    near = bits - 1
    return [far + [near, 0, bits], [0, near] + far + [bits]]


def gather_kernel(bits, cuts, pack_ref, tok_ref, table_ref, out_ref, toks_ref, tables_ref, local_sem, send_sem, recv_sem, tok_sem):
    coords = coordinates(bits)
    dims = bits + 1
    greet([partner(d, bits) for d in range(dims)])
    other = partner(0, bits)
    seq = coords[0]
    extras = []
    for n, (src, dst) in enumerate(((tok_ref, toks_ref), (table_ref, tables_ref))):
        copy = pltpu.make_async_remote_copy(
            src, dst.at[seq], tok_sem.at[0, n], tok_sem.at[1, n], device_id=other, device_id_type=MESH
        )
        keep = pltpu.make_async_copy(src, dst.at[seq], tok_sem.at[2, n])
        copy.start()
        keep.start()
        extras += [copy, keep]
    own = pltpu.make_async_copy(pack_ref, out_ref.at[tuple(coords)], local_sem)
    own.start()
    orders = gather_orders(bits)
    done = [[] for _ in cuts]
    flying = [None for _ in cuts]
    sent = []
    for step in range(dims):
        for part, (start, rows) in enumerate(cuts):
            dim = orders[part][step]
            if step == 0:
                src = pack_ref.at[pl.ds(start, rows)]
                dst = out_ref.at[tuple(coords) + (pl.ds(start, rows),)]
            else:
                if step == 1 and part == 0:
                    own.wait()
                flying[part].wait_recv()
                where = tuple(slice(None) if d in done[part] else coords[d] for d in range(dims))
                src = out_ref.at[where + (pl.ds(start, rows),)]
                dst = src
            copy = pltpu.make_async_remote_copy(
                src,
                dst,
                send_sem.at[part, step],
                recv_sem.at[part, step],
                device_id=partner(dim, bits),
                device_id_type=MESH,
            )
            copy.start()
            sent.append(copy)
            flying[part] = copy
            done[part].append(dim)
    for copy in flying:
        copy.wait_recv()
    for copy in sent:
        copy.wait_send()
    for copy in extras:
        copy.wait()


def gather_all(pack, tokens, table, bits):
    rows, columns = pack.shape
    cuts = [(0, 48), (48, rows - 48)] if rows > 64 else [(0, rows)]
    lead = (2,) * (bits + 1)
    any_spec = pl.BlockSpec(memory_space=pl.ANY)
    return pl.pallas_call(
        functools.partial(gather_kernel, bits, cuts),
        out_shape=(
            jax.ShapeDtypeStruct(lead + (rows, columns), BF16),
            jax.ShapeDtypeStruct((2,) + tokens.shape, BF16),
            jax.ShapeDtypeStruct((2,) + table.shape, BF16),
        ),
        in_specs=[any_spec] * 3,
        out_specs=(any_spec,) * 3,
        scratch_shapes=[
            pltpu.SemaphoreType.DMA,
            pltpu.SemaphoreType.DMA((len(cuts), bits + 1)),
            pltpu.SemaphoreType.DMA((len(cuts), bits + 1)),
            pltpu.SemaphoreType.DMA((3, 2)),
        ],
        compiler_params=pltpu.CompilerParams(collective_id=0, has_side_effects=True, vmem_limit_bytes=VMEM_LIMIT),
    )(pack, tokens, table)


def reduce_kernel(bits, parts, *refs):
    ins, table_ref, far_ref = refs[:parts], refs[parts], refs[parts + 1]
    outs, table_out, far_out = refs[parts + 2 : 2 * parts + 2], refs[2 * parts + 2], refs[2 * parts + 3]
    rest = list(refs[2 * parts + 4 :])
    dims = bits + 1
    landed = [rest[p * dims : (p + 1) * dims] for p in range(parts)]
    rest = rest[parts * dims :]
    sums = [rest[p * bits : (p + 1) * bits] for p in range(parts)]
    rest = rest[parts * bits :]
    table_landed, table_sums, send_sem, recv_sem, table_sem, far_sem = rest
    coords = coordinates(bits)
    greet([partner(d, bits) for d in range(dims)])
    far_copy = pltpu.make_async_remote_copy(
        far_ref, far_out, far_sem.at[0], far_sem.at[1], device_id=partner(0, bits), device_id_type=MESH
    )
    far_copy.start()
    orders = [list(reversed(order)) for order in gather_orders(bits)]
    held = list(ins)
    left = [list(range(dims)) for _ in range(parts)]
    sent = [far_copy]
    table_now = table_ref
    for step in range(dims):
        flying = []
        for part in range(parts):
            dim = orders[part][step]
            spot = left[part].index(dim)
            whole = (slice(None),) * spot
            copy = pltpu.make_async_remote_copy(
                held[part].at[whole + (1 - coords[dim],)],
                landed[part][step],
                send_sem.at[part, step],
                recv_sem.at[part, step],
                device_id=partner(dim, bits),
                device_id_type=MESH,
            )
            copy.start()
            sent.append(copy)
            flying.append((copy, whole, dim))
        small = pltpu.make_async_remote_copy(
            table_now,
            table_landed.at[step],
            table_sem.at[0, step],
            table_sem.at[1, step],
            device_id=partner(step, bits),
            device_id_type=MESH,
        )
        small.start()
        sent.append(small)
        for part, (copy, whole, dim) in enumerate(flying):
            copy.wait_recv()
            total = held[part][whole + (coords[dim],)].astype(F32) + landed[part][step][...].astype(F32)
            left[part].remove(dim)
            if step == dims - 1:
                outs[part][...] = total
            else:
                sums[part][step][...] = total.astype(BF16)
                held[part] = sums[part][step]
        small.wait_recv()
        total = table_now[...] + table_landed[step]
        if step == dims - 1:
            table_out[...] = total
        else:
            table_sums[step] = total
            table_now = table_sums.at[step]
    far_copy.wait_recv()
    for copy in sent:
        copy.wait_send()


def reduce_all(parts, table, far, bits):
    dims = bits + 1
    vmem = pl.BlockSpec(memory_space=pltpu.VMEM)
    count = len(parts)
    scratch = []
    for part in parts:
        scratch += [pltpu.VMEM((2,) * (dims - 1 - s) + part.shape[-2:], BF16) for s in range(dims)]
    for part in parts:
        scratch += [pltpu.VMEM((2,) * (dims - 1 - s) + part.shape[-2:], BF16) for s in range(dims - 1)]
    scratch += [
        pltpu.VMEM((dims,) + table.shape, F32),
        pltpu.VMEM((dims,) + table.shape, F32),
        pltpu.SemaphoreType.DMA((count, dims)),
        pltpu.SemaphoreType.DMA((count, dims)),
        pltpu.SemaphoreType.DMA((2, dims)),
        pltpu.SemaphoreType.DMA((2,)),
    ]
    return pl.pallas_call(
        functools.partial(reduce_kernel, bits, count),
        out_shape=tuple(jax.ShapeDtypeStruct(part.shape[-2:], F32) for part in parts)
        + (jax.ShapeDtypeStruct(table.shape, F32), jax.ShapeDtypeStruct(far.shape, BF16)),
        in_specs=[vmem] * (count + 2),
        out_specs=(vmem,) * (count + 2),
        scratch_shapes=scratch,
        compiler_params=pltpu.CompilerParams(collective_id=1, has_side_effects=True, vmem_limit_bytes=VMEM_LIMIT),
    )(*parts, table, far)


def contract(a, b, on_a, on_b):
    return lax.dot_general(a, b, (((on_a,), (on_b,)), ((), ())), preferred_element_type=F32)


GELU_SCALE = 0.7978845608028654


def expert_kernel(
    chips, buf_ref, grad_ref, w_in_ref, w_out_ref, slots_ref, gslots_ref, wgrad_ref,
    rows_x, rows_g, act_ref, gpre_ref, part_ref, sib_ref, ret_ref,
    in_sem, fwd_sem, sib_sem, out_sem,
):
    seq, shard = lax.axis_index("seq"), lax.axis_index("shard")
    chip, core = shard // 2, shard % 2
    sibling = (seq, shard + 1 - 2 * core)
    capacity, width = buf_ref.shape[1:]
    hidden = w_in_ref.shape[1]

    def device_of(other):
        return (seq, 2 * other + core)

    greet([device_of((chip + j) % chips) for j in range(1, chips)] + [sibling])
    pairs = ((buf_ref, rows_x), (grad_ref, rows_g))
    sent = []
    copies = {}
    for j in range(1, chips):
        to = (chip + j) % chips
        for n, (src, dst) in enumerate(pairs):
            copy = pltpu.make_async_remote_copy(
                src.at[to], dst.at[chip, core], in_sem.at[0, n, j], in_sem.at[1, n, j],
                device_id=device_of(to), device_id_type=MESH,
            )
            copy.start()
            copies[n, j] = copy
            sent.append(copy)
    for n, (src, dst) in enumerate(pairs):
        dst[chip, core] = src[chip]
    forwards = []
    for j in range(chips):
        source = (chip + chips - j) % chips
        for n, (src, dst) in enumerate(pairs):
            if j:
                copies[n, j].wait_recv()
            copy = pltpu.make_async_remote_copy(
                dst.at[source, core], dst.at[source, core], fwd_sem.at[0, n, j], fwd_sem.at[1, n, j],
                device_id=sibling, device_id_type=MESH,
            )
            copy.start()
            forwards.append(copy)
            sent.append(copy)
    for copy in forwards:
        copy.wait_recv()

    group = max(1, 256 // (2 * capacity))
    block = group * 2 * capacity
    piece = 512

    @pl.loop(0, chips // group)
    def _(t):
        x = rows_x[pl.ds(t * group, group)].reshape(block, width)
        g = rows_g[pl.ds(t * group, group)].reshape(block, width)
        out_sum = jnp.zeros((block, width), F32)
        half_sum = jnp.zeros((block, width), F32)
        where = pl.ds(pl.multiple_of(t * block, block), block)
        for h in range(hidden // piece):
            cols = pl.ds(h * piece, piece)
            pre = jnp.dot(x, w_in_ref[:, cols], preferred_element_type=F32)
            gact = contract(g, w_out_ref[cols, :], 1, 1)
            square = pre * pre
            t_val = jnp.tanh(GELU_SCALE * (pre + 0.044715 * square * pre))
            act = (0.5 * pre * (1.0 + t_val)).astype(BF16)
            slope = 0.5 * (1.0 + t_val) + 0.5 * pre * (1.0 - t_val * t_val) * (
                GELU_SCALE * (1.0 + 0.134145 * square)
            )
            gpre = (gact * slope).astype(BF16)
            act_ref[where, cols] = act
            gpre_ref[where, cols] = gpre
            out_sum += jnp.dot(act, w_out_ref[cols, :], preferred_element_type=F32)
            half_sum += contract(gpre, w_in_ref[:, cols], 1, 1)
        out_b = out_sum.astype(BF16).reshape(group, 2, capacity, width)
        half_b = half_sum.astype(BF16).reshape(group, 2, capacity, width)
        for u in range(2):
            part_ref[0, u, pl.ds(t * group, group)] = out_b[:, u]
            part_ref[1, u, pl.ds(t * group, group)] = half_b[:, u]

    swaps = []
    for n in range(2):
        copy = pltpu.make_async_remote_copy(
            part_ref.at[n, 1 - core], sib_ref.at[n], sib_sem.at[0, n], sib_sem.at[1, n],
            device_id=sibling, device_id_type=MESH,
        )
        copy.start()
        swaps.append(copy)
        sent.append(copy)
    returns = []
    outs = (slots_ref, gslots_ref)
    for n in range(2):
        swaps[n].wait_recv()
        ret_ref[n] = (part_ref[n, core].astype(F32) + sib_ref[n].astype(F32)).astype(BF16)
        for j in range(1, chips):
            to = (chip + j) % chips
            copy = pltpu.make_async_remote_copy(
                ret_ref.at[n, to], outs[n].at[chip], out_sem.at[0, n, j], out_sem.at[1, n, j],
                device_id=device_of(to), device_id_type=MESH,
            )
            copy.start()
            returns.append(copy)
            sent.append(copy)
        outs[n][chip] = ret_ref[n, chip]
    all_x = rows_x[...].reshape(-1, width)
    all_g = rows_g[...].reshape(-1, width)
    side = hidden // 2
    for h in range(2):
        cols = pl.ds(h * side, side)
        wgrad_ref[h, 0] = contract(all_x, gpre_ref[:, cols], 0, 0).astype(BF16)
        wgrad_ref[h, 1] = contract(act_ref[:, cols], all_g, 0, 0).astype(BF16)
    for copy in returns:
        copy.wait_recv()
    for copy in sent:
        copy.wait_send()


def run_experts(buffer, grad_slots, w_in, w_out):
    chips, capacity, width = buffer.shape
    hidden = w_in.shape[1]
    rows = chips * 2 * capacity
    vmem = pl.BlockSpec(memory_space=pltpu.VMEM)
    return pl.pallas_call(
        functools.partial(expert_kernel, chips),
        out_shape=(
            jax.ShapeDtypeStruct(buffer.shape, BF16),
            jax.ShapeDtypeStruct(buffer.shape, BF16),
            jax.ShapeDtypeStruct((2, 2, width, hidden // 2), BF16),
        ),
        in_specs=[vmem] * 4,
        out_specs=(vmem,) * 3,
        scratch_shapes=[
            pltpu.VMEM((chips, 2, capacity, width), BF16),
            pltpu.VMEM((chips, 2, capacity, width), BF16),
            pltpu.VMEM((rows, hidden), BF16),
            pltpu.VMEM((rows, hidden), BF16),
            pltpu.VMEM((2, 2, chips, capacity, width), BF16),
            pltpu.VMEM((2, chips, capacity, width), BF16),
            pltpu.VMEM((2, chips, capacity, width), BF16),
            pltpu.SemaphoreType.DMA((2, 2, chips)),
            pltpu.SemaphoreType.DMA((2, 2, chips)),
            pltpu.SemaphoreType.DMA((2, 2)),
            pltpu.SemaphoreType.DMA((2, 2, chips)),
        ],
        compiler_params=pltpu.CompilerParams(collective_id=2, has_side_effects=True, vmem_limit_bytes=VMEM_LIMIT),
    )(buffer, grad_slots, w_in, w_out)


def rms_parts(values):
    inverse = lax.rsqrt(jnp.mean(values * values, axis=-1, keepdims=True) + EPS)
    return (values * inverse, inverse)


def rms_back(grad_normed, normed, inverse):
    return inverse * (grad_normed - normed * jnp.mean(grad_normed * normed, axis=-1, keepdims=True))


def spread_offsets(per_offset, block_rows, columns):
    heads_here = per_offset.shape[0]
    period = block_rows + columns
    padded = jnp.pad(per_offset, ((0, 0), (0, 1)))
    tiled = jnp.tile(padded, (1, block_rows))[:, : block_rows * (period - 1)]
    return tiled.reshape(heads_here, block_rows, period - 1)[:, :, block_rows - 1 :]


def offset_sums(grid):
    heads_here, block_rows, columns = grid.shape
    period = block_rows + columns
    widened = jnp.pad(grid, ((0, 0), (0, 0), (block_rows - 1, 0)))
    flat_grid = widened.reshape(heads_here, block_rows * (period - 1))
    flat_grid = jnp.pad(flat_grid, ((0, 0), (0, block_rows)))
    return jnp.sum(flat_grid.reshape(heads_here, block_rows, period), axis=1)[:, : period - 1]


def heads_of(matrix):
    return matrix.reshape(matrix.shape[0], -1, HEAD_DIM)


def local(
    devices_along_shard, tokens_in, w_query, w_key, w_value, output_weight, gain_attn, gain_moe, router_weight,
    bias_table, w_expert_in, w_expert_out, expert_id, slot_id, bucket_id, cotangent,
):
    bits = devices_along_shard.bit_length() - 1
    devices = 2 * devices_along_shard
    seq = lax.axis_index("seq")
    rows, width = w_query.shape
    experts = router_weight.shape[1]
    tokens_here = tokens_in.shape[1]
    length = 2 * tokens_here
    capacity = 2 * max(1, 5 * tokens_here // (8 * experts))
    slots = round_up(capacity, 16)
    pack_rows = round_up(4 * rows + 1, 16)
    heads_side, buckets = bias_table.shape

    extra = jnp.concatenate([router_weight.reshape(-1), gain_attn, gain_moe])
    extra = jnp.pad(extra, (0, width - extra.shape[0]))[None]
    pack = jnp.concatenate([w_query, w_key, w_value, output_weight, extra], axis=0)
    pack = jnp.pad(pack, ((0, pack_rows - pack.shape[0]), (0, 0)))
    table_tile = jnp.pad(bias_table, ((0, 16 - heads_side), (0, 128 - buckets)))
    gathered, both_tokens, both_tables = gather_all(pack, tokens_in[0], table_tile, bits)
    gathered = gathered.reshape(devices, pack_rows, width)
    full_query, full_key, full_value, full_output = (
        gathered[:, n * rows : (n + 1) * rows].reshape(width, width) for n in range(4)
    )
    extra = gathered[:, 4 * rows]
    cut = rows * experts
    full_router = extra[:, :cut].reshape(width, experts)
    full_gain_attn = extra[:, cut : cut + rows].reshape(width).astype(F32)
    full_gain_moe = extra[:, cut + rows : cut + 2 * rows].reshape(width).astype(F32)
    full_table = both_tables[:, :heads_side, :buckets].reshape(2 * heads_side, buckets)

    def mine(array):
        return lax.dynamic_slice_in_dim(array, seq * tokens_here, tokens_here, 0)

    inputs = tokens_in[0].astype(F32)
    normed_all, _ = rms_parts(both_tokens.reshape(length, width).astype(F32))
    normed_attn, inverse_attn = rms_parts(inputs)
    hidden_all = (normed_all * full_gain_attn).astype(BF16)
    hidden_own = (normed_attn * full_gain_attn).astype(BF16)
    queries = heads_of(jnp.dot(hidden_own, full_query, preferred_element_type=F32).astype(BF16))
    keys = heads_of(jnp.dot(hidden_all, full_key, preferred_element_type=F32).astype(BF16))
    values = heads_of(jnp.dot(hidden_all, full_value, preferred_element_type=F32).astype(BF16))

    bucket_onehot = (jnp.arange(buckets, dtype=jnp.int32)[:, None] == bucket_id[None, :]).astype(BF16)
    onehot_here = lax.dynamic_slice_in_dim(
        bucket_onehot, tokens_here * (1 - seq), tokens_here + length - 1, 1
    )
    per_offset = jnp.dot(full_table, onehot_here, preferred_element_type=F32)
    scores = jnp.einsum("qhd,khd->hqk", queries, keys, preferred_element_type=F32)
    scores = scores + spread_offsets(per_offset, tokens_here, length)
    weights = jnp.exp(scores - jnp.max(scores, axis=-1, keepdims=True))
    probs = weights / jnp.sum(weights, axis=-1, keepdims=True)
    probs_low = probs.astype(BF16)
    mixed = jnp.einsum("hqk,khd->qhd", probs_low, values, preferred_element_type=F32)
    mixed = mixed.reshape(tokens_here, width).astype(BF16)

    after_attn = inputs + jnp.dot(mixed, full_output, preferred_element_type=F32)
    normed_moe, inverse_moe = rms_parts(after_attn)
    hidden_moe = (normed_moe * full_gain_moe).astype(BF16)
    router_logits = jnp.dot(hidden_moe, full_router, preferred_element_type=F32)
    gate_weights = jnp.exp(router_logits - jnp.max(router_logits, axis=-1, keepdims=True))
    gate_probs = gate_weights / jnp.sum(gate_weights, axis=-1, keepdims=True)
    chosen = (expert_id[0][:, None] == jnp.arange(experts, dtype=jnp.int32)[None, :]).astype(F32)
    picked = jnp.sum(gate_probs * chosen, axis=-1, keepdims=True)
    slot_of = jnp.where(slot_id[0] >= 0, expert_id[0] * slots + slot_id[0], -1)
    dispatch = (slot_of[:, None] == jnp.arange(experts * slots, dtype=jnp.int32)[None, :]).astype(BF16)
    grad_out = cotangent[0].astype(F32)
    scaled = (picked * grad_out).astype(BF16)
    buffer = contract(dispatch, hidden_moe, 0, 0).astype(BF16)
    grad_slots = contract(dispatch, scaled, 0, 0).astype(BF16)
    expert_slots, grad_buffer, expert_grads = run_experts(
        buffer.reshape(experts, slots, width),
        grad_slots.reshape(experts, slots, width),
        w_expert_in[0],
        w_expert_out[0],
    )
    leaving = lax.dynamic_index_in_dim(expert_grads, 1 - seq, 0, keepdims=False)
    arriving = lax.ppermute(leaving, "seq", [(0, 1), (1, 0)])

    combined = jnp.dot(dispatch, expert_slots.reshape(-1, width), preferred_element_type=F32)
    block_out = after_attn + picked * combined
    grad_picked = jnp.sum(grad_out * combined, axis=-1, keepdims=True)
    grad_gates = chosen * grad_picked
    grad_logits = gate_probs * (grad_gates - jnp.sum(gate_probs * grad_gates, axis=-1, keepdims=True))
    grad_logits = grad_logits.astype(BF16)
    grad_router = contract(hidden_moe, grad_logits, 0, 0)
    grad_hidden_moe = contract(grad_logits, full_router, 1, 1)
    grad_hidden_moe = grad_hidden_moe + jnp.dot(
        dispatch, grad_buffer.reshape(-1, width), preferred_element_type=F32
    )
    grad_gain_moe = jnp.sum(grad_hidden_moe * normed_moe, axis=0)
    grad_mid = grad_out + rms_back(grad_hidden_moe * full_gain_moe, normed_moe, inverse_moe)
    grad_branch = grad_mid.astype(BF16)
    grad_output = contract(mixed, grad_branch, 0, 0)
    grad_mixed = heads_of(contract(grad_branch, full_output, 1, 1).astype(BF16))

    grad_probs = jnp.einsum("qhd,khd->hqk", grad_mixed, values, preferred_element_type=F32)
    centre = jnp.sum(probs * grad_probs, axis=-1, keepdims=True)
    grad_scores = (probs * (grad_probs - centre)).astype(BF16)
    grad_q = jnp.einsum("hqk,khd->qhd", grad_scores, keys, preferred_element_type=F32)
    grad_k = jnp.einsum("hqk,qhd->khd", grad_scores, queries, preferred_element_type=F32)
    grad_v = jnp.einsum("hqk,qhd->khd", probs_low, grad_mixed, preferred_element_type=F32)
    grad_q = grad_q.reshape(tokens_here, width).astype(BF16)
    grad_k = grad_k.reshape(length, width).astype(BF16)
    grad_v = grad_v.reshape(length, width).astype(BF16)
    grad_offset = offset_sums(grad_scores.astype(F32))
    grad_table = jnp.einsum(
        "ho,bo->hb", grad_offset, onehot_here.astype(F32), precision=lax.Precision.HIGHEST
    )
    grad_table = jnp.pad(grad_table, ((0, 16 - 2 * heads_side), (0, 128 - buckets)))

    back_query = contract(grad_q, full_query, 1, 1)
    back_all = contract(grad_k, full_key, 1, 1) + contract(grad_v, full_value, 1, 1)
    grad_gain_attn = jnp.sum(back_query * normed_attn, axis=0) + jnp.sum(back_all * normed_all, axis=0)
    far = lax.dynamic_slice_in_dim(back_all, (1 - seq) * tokens_here, tokens_here, 0).astype(BF16)

    def by_device(matrix):
        return matrix.reshape(devices, rows, width).astype(BF16)

    extra = jnp.concatenate(
        [
            grad_router.reshape(devices, rows * experts),
            grad_gain_attn.reshape(devices, rows),
            grad_gain_moe.reshape(devices, rows),
        ],
        axis=1,
    )
    extra = jnp.pad(extra, ((0, 0), (0, width - extra.shape[1])))[:, None].astype(BF16)
    pieces = [
        by_device(contract(hidden_own, grad_q, 0, 0)),
        by_device(contract(hidden_all, grad_k, 0, 0)),
        by_device(contract(hidden_all, grad_v, 0, 0)),
        by_device(grad_output),
        extra,
    ]
    lead = (2,) * (bits + 1)

    def joined(some):
        part = jnp.concatenate(some, axis=1)
        part = jnp.pad(part, ((0, 0), (0, round_up(part.shape[1], 16) - part.shape[1]), (0, 0)))
        return part.reshape(lead + part.shape[1:])

    parts = [joined(pieces[:2]), joined(pieces[2:])] if rows % 8 == 0 else [joined(pieces)]
    *sums, table_sum, far_sum = reduce_all(parts, grad_table, far, bits)
    total = jnp.concatenate([sums[0][: 2 * rows], *sums[1:]], axis=0) if len(sums) > 1 else sums[0]
    share = total[4 * rows]

    grad_hidden_attn = back_query + mine(back_all) + far_sum.astype(F32)
    grad_tokens = grad_mid + rms_back(grad_hidden_attn * full_gain_attn, normed_attn, inverse_attn)
    kept = lax.dynamic_index_in_dim(expert_grads, seq, 0, keepdims=False)
    expert_sum = kept.astype(F32) + arriving.astype(F32)
    return (
        block_out.astype(BF16)[None],
        grad_tokens[None],
        total[:rows],
        total[rows : 2 * rows],
        total[2 * rows : 3 * rows],
        total[3 * rows : 4 * rows],
        share[cut : cut + rows],
        share[cut + rows : cut + 2 * rows],
        share[:cut].reshape(rows, experts),
        lax.dynamic_slice_in_dim(table_sum[:, :buckets], seq * heads_side, heads_side, 0),
        expert_sum[0][None],
        expert_sum[1][None],
    )


def solution(mesh):
    return jax.shard_map(
        functools.partial(local, mesh.shape["shard"]),
        mesh=mesh,
        in_specs=(
            P("shard", "seq", None),
            P(("seq", "shard"), None),
            P(("seq", "shard"), None),
            P(("seq", "shard"), None),
            P(("seq", "shard"), None),
            P(("seq", "shard")),
            P(("seq", "shard")),
            P(("seq", "shard"), None),
            P("seq", None),
            P("shard", None, None),
            P("shard", None, None),
            P("shard", "seq"),
            P("shard", "seq"),
            P(),
            P("shard", "seq", None),
        ),
        out_specs=(
            P("shard", "seq", None),
            P("shard", "seq", None),
            P(("seq", "shard"), None),
            P(("seq", "shard"), None),
            P(("seq", "shard"), None),
            P(("seq", "shard"), None),
            P(("seq", "shard")),
            P(("seq", "shard")),
            P(("seq", "shard"), None),
            P("seq", None),
            P("shard", None, "seq"),
            P("shard", "seq", None),
        ),
        check_vma=False,
    )
```

time: 682 us -> 275 us (0.40)
  waiting for transfers between devices: 292 us -> 0.01 us
  blocking collectives: 222 us -> 0 us
  Pallas kernels: 0 us -> 182 us
  matrix products: 48.6 us -> 27.8 us
  starting transfers between devices: 19.5 us -> 1.49 us
  between operations: 15.5 us -> 1.55 us
  local copies, waits for them, and re-layouts: 58.3 us -> 47.4 us
  other arithmetic: 21.8 us -> 14.4 us
    pallas_call x0 -> x3, Pallas kernels: none -> 182 us  [the longest x1 70.2 us: reduce_all(): pl.pallas_call(functools.partial(reduce_kernel, bits, count), out_shape=t...]
    all_gather x4 -> x0, waiting for transfers between devices: 134 us -> none  [the longest x1 54.2 us: local(): lax.all_gather(w_key, ('seq', 'shard'), axis=0, tiled=True)]
    reduce_scatter x4 -> x0, waiting for transfers between devices: 128 us -> none  [the longest x1 103 us: local(): lax.psum_scatter(grad_output, ('seq', 'shard'), scatter_dimension=0, tile...]
    unnamed x2 -> x0, blocking collectives: 80.7 us -> none
    all_to_all x3 -> x0, blocking collectives: 62.5 us -> none  [the longest x2 41.6 us: to_holders(): lax.all_to_all(outgoing.reshape(2 * experts, capacity, features), 'shard'...]
    all_gather x1 -> x0, blocking collectives: 45.1 us -> none  [local(): lax.all_gather(router_weight, ('seq', 'shard'), axis=0, tiled=True)]
    psum x1 -> x0, blocking collectives: 33.3 us -> none  [local(): grad_table = lax.psum(grad_table, 'shard')]
    all_to_all x5 -> x0, waiting for transfers between devices: 27.1 us -> none  [the longest x2 15.2 us: to_sources(): lax.all_to_all(partial_value, 'shard', split_axis=0, concat_axis=0, tiled...]
  transfers between devices with their start and end apart: 13 -> 1, of which waited for: 9 -> 0; matrix products, arithmetic and copies ran while one was open for 14% -> 14% of each run, Pallas kernels for 0% -> 26%
where the time goes in v1:
time: 275 us; the launch traced here: 274 us
  Pallas kernels  182 us (66%)
  local copies, waits for them, and re-layouts  47.4 us (17%)
  matrix products  27.8 us (10%)
  other arithmetic  14.4 us (5%)
    pallas_call x1, Pallas kernels, reduce_all(): pl.pallas_call(functools.partial(reduce_kernel, bits, count), out_shape=t...  70.2 us
    pallas_call x1, Pallas kernels, gather_all(): pl.pallas_call(functools.partial(gather_kernel, bits, cuts), out_shape=(j...  61.6 us
    pallas_call x1, Pallas kernels, run_experts(): pl.pallas_call(functools.partial(expert_kernel, chips), out_shape=(jax.Sh...  50 us
    unnamed x134, local copies, waits for them, and re-layouts  12.9 us
    dot_general x12, matrix products, contract(): lax.dot_general(a, b, (((on_a,), (on_b,)), ((), ())), preferred_element_t...  7.53 us
    dot_general x1, matrix products, local(): jnp.einsum('hqk,qhd->khd', probs_low, grad_mixed, preferred_element_type=...  5.63 us
  transfers between devices with their start and end apart: 1, of which 0 were waited for; matrix products, arithmetic and copies ran while one was open for 14% of the time, Pallas kernels for 26%

profile of v1, /device:TPU:0, one launch (start us, length us, event | category | flops | bytes accessed | tf_op | source)
XLA Modules:
  0.0 274.4 jit_solution(8842821865917210638)
XLA Ops:
  6.0 1.3 pad.41.table_ref
  7.3 61.6 %shard_map.238 = (bf16[2,2,2,2,2,112,768]{6,5,4,3,2,1,0:T(8,128)(2,1)}, bf16[2,128,768]{2,1,0:T(8,128)(2,1)}, bf16[2,16,128]{2,1,0:T(8,128)(2,1)}) custom-call(bf16[112,768]{1,0:T(8,128)(2,1)} %pad.40.pack_ref, bf16[128,768]{1,0:T(8,128)(2,1)} %bitcast.161, bf16[16,128]{1,0:T(8,128)(2,1)} %pad.41.table_ref), custom_call_target="tpu_custom_call" | custom-call | tf_op jit(solution)/shard_map/pallas_call | solution.py:107
  69.0 1.1 slice.101
  70.0 4.3 %fusion.68 = (bf16[32,24,768]{2,1,0:T(8,128)(2,1)}, bf16[32,24,768]{2,1,0:T(8,128)(2,1)}, bf16[32,24,768]{2,1,0:T(8,128)(2,1)}, bf16[32,24,768]{2,1,0:T(8,128)(2,1)S(1)}) fusion(bf16[32,112,768]{2,1,0:T(8,128)(2,1)} %bitcast.164), kind=kLoop, calls=%fused_computation.137 | loop fusion | bytes 9437184 | tf_op jit(solution)/shard_map/slice | solution.py:430
  76.8 0.9 copy.45
  78.4 1.8 copy.64
  80.5 3.6 %reshape.270 = f32[12,128,383]{2,1,0:T(8,128)} reshape(f32[12,49024]{1,0:T(8,128)S(1)} %slice.106) | data formatting | bytes 4706304 | tf_op jit(solution)/shard_map/reshape | solution.py:390
  84.1 1.7 convolution_convert_fusion.13
  86.7 2.5 slice_add_fusion
  89.2 1.4 fusion.72
  90.9 4.8 %convolution_convert_fusion.12 = bf16[12,64,128]{2,1,0:T(8,128)(2,1)S(1)} fusion(bf16[256,12,64]{0,2,1:T(8,128)(2,1)S(1)} %bitcast.188, f32[12,128]{1,0:T(8,128)S(1)} %get-tuple-element.80, f32[12,128,256]{2,1,0:T(8,128)} %copy-done.6), kind=kOutput, calls=%fused_computation.32 | convolution fusion | flops 51611392 | bytes 2168832 | tf_op jit(solution)/shard_map/hqk,khd->qhd/dot_general | solution.py:461
  97.3 1.1 convolution_convert_fusion.7
  100.4 1.8 convolution_convert_fusion.6
  102.2 50.0 %shard_map.239 = (bf16[8,32,768]{2,1,0:T(8,128)(2,1)}, bf16[8,32,768]{2,1,0:T(8,128)(2,1)}, bf16[2,2,768,768]{3,2,1,0:T(8,128)(2,1)}) custom-call(bf16[8,32,768]{2,1,0:T(8,128)(2,1)} %bitcast.183, bf16[8,32,768]{2,1,0:T(8,128)(2,1)} %bitcast.182, bf16[768,1536]{1,0:T(8,128)(2,1)} %bitcast.173, bf16[1536,768]{1,0:T(8,128)(2,1)} %bitcast.174), custom_call_target="tpu_custom_call" | custom-call | tf_op jit(solution)/shard_map/pallas_call | solution.py:350
  152.2 3.3 %dynamic-slice_bitcast_fusion = bf16[2,768,768]{2,1,0:T(8,128)(2,1)} fusion(bf16[2,2,768,768]{3,2,1,0:T(8,128)(2,1)} %get-tuple-element.31, s32[]{:T(128)S(6)} %select_n.33), kind=kLoop, calls=%fused_computation.10 | loop fusion | bytes 4718596 | tf_op jit(solution)/shard_map/jit(dynamic_index_in_dim)/squeeze | solution.py:484
  155.5 1.5 collective-permute-start
  157.7 0.9 multiply_reduce_fusion.3
  160.9 5.6 %convolution_convert_fusion.4 = bf16[12,64,256]{2,1,0:T(8,128)(2,1)} fusion(bf16[128,12,64]{0,2,1:T(8,128)(2,1)} %bitcast.191, f32[12,128]{1,0:T(8,128)S(1)} %copy-done.33, f32[12,128,256]{2,1,0:T(8,128)} %copy-done.6), kind=kOutput, calls=%fused_computation.22 | convolution fusion | flops 51709696 | bytes 2168832 | tf_op jit(solution)/shard_map/hqk,qhd->khd/dot_general | solution.py:509
  166.5 1.8 multiply_reduce_fusion
  170.9 1.5 pad.45
  174.5 0.9 copy.51
  178.0 3.9 %reshape.282 = bf16[12,49024]{1,0:T(8,128)(2,1)S(1)} reshape(bf16[12,128,383]{2,1,0:T(8,128)(2,1)} %pad.45) | data formatting | bytes 2353152 | tf_op jit(solution)/shard_map/reshape | solution.py:397
  185.0 1.6 pad_maximum_fusion
  189.0 1.8 fusion.5
  190.9 70.2 %shard_map.240 = (f32[48,768]{1,0:T(8,128)}, f32[64,768]{1,0:T(8,128)}, f32[16,128]{1,0:T(8,128)}, bf16[128,768]{1,0:T(8,128)(2,1)}) custom-call(bf16[2,2,2,2,2,48,768]{6,5,4,3,2,1,0:T(8,128)(2,1)} %bitcast.162, bf16[2,2,2,2,2,64,768]{6,5,4,3,2,1,0:T(8,128)(2,1)} %bitcast.150, f32[16,128]{1,0:T(8,128)} %pad.47.refs_2_, ...), custom_call_target="tpu_custom_call" | custom-call | tf_op jit(solution)/shard_map/pallas_call | solution.py:212
  262.6 1.3 constant_dynamic-slice_fusion
  263.9 1.1 fusion.14
  265.0 1.3 slice_bitcast_fusion
  266.4 1.7 fusion.70
  268.1 0.9 fusion.18
  269.0 2.9 %convert_add_fusion = f32[2,768,768]{2,1,0:T(8,128)S(1)} fusion(bf16[2,768,768]{2,1,0:T(8,128)(2,1)} %collective-permute-done, bf16[2,2,768,768]{3,2,1,0:T(8,128)(2,1)} %get-tuple-element.31, s32[]{:T(128)S(6)} %select_n.32), kind=kLoop, calls=%fused_computation.5 | loop fusion | flops 3538944 | bytes 9437188 | tf_op jit(solution)/shard_map/add | solution.py:558
  271.9 2.5 fusion.69
  (201 shorter events, 30.1 us)
Async XLA Ops:
  70.0 4.3 %copy-start.5 = (bf16[1,128,768]{2,1,0:T(8,128)(2,1)S(1)}, bf16[1,128,768]{2,1,0:T(8,128)(2,1)}, u32[]{:S(2)}) copy-start(bf16[1,128,768]{2,1,0:T(8,128)(2,1)} %param.15) | copy-start | bytes 589828
  70.0 4.6 %copy-start.8 = (bf16[2,128,768]{2,1,0:T(8,128)(2,1)S(1)}, bf16[2,128,768]{2,1,0:T(8,128)(2,1)}, u32[]{:S(2)}) copy-start(bf16[2,128,768]{2,1,0:T(8,128)(2,1)} %get-tuple-element.22) | copy-start | bytes 1179652
  74.3 2.5 copy-start.3
  75.5 2.2 copy-start.59
  75.5 2.2 copy-start.60
  84.1 1.9 copy-start.1
  84.1 2.0 copy-start.16
  84.1 2.4 copy-start.50
  86.0 3.2 %copy-start.17 = (bf16[128,768]{0,1:T(8,128)(2,1)}, bf16[128,768]{0,1:T(8,128)(2,1)S(1)}, u32[]{:S(2)}) copy-start(bf16[128,768]{0,1:T(8,128)(2,1)S(1)} %copy.46) | copy-start | bytes 589828
  86.7 2.5 copy-start.10
  89.2 1.7 copy-start.6
  89.2 1.7 copy-start.28
  90.9 4.8 %copy-start.32 = (f32[12,128]{1,0:T(8,128)}, f32[12,128]{1,0:T(8,128)S(1)}, u32[]{:S(2)}) copy-start(f32[12,128]{1,0:T(8,128)S(1)} %get-tuple-element.80) | copy-start | bytes 18436
  90.9 4.9 %copy-start.2 = (bf16[32,24,768]{2,1,0:T(8,128)(2,1)S(1)}, bf16[32,24,768]{2,1,0:T(8,128)(2,1)}, u32[]{:S(2)}) copy-start(bf16[32,24,768]{2,1,0:T(8,128)(2,1)} %get-tuple-element.58) | copy-start | bytes 3538948
  95.8 4.6 %copy-start.21 = (bf16[1,128,768]{2,1,0:T(8,128)(2,1)S(1)}, bf16[1,128,768]{2,1,0:T(8,128)(2,1)}, u32[]{:S(2)}) copy-start(bf16[1,128,768]{2,1,0:T(8,128)(2,1)} %param.29) | copy-start | bytes 589828
  98.6 58.8 %copy-start.37 = (f32[128]{0:T(128)}, f32[128]{0:T(128)S(1)}, u32[]{:S(2)}) copy-start(f32[128]{0:T(128)S(1)} %get-tuple-element.84) | copy-start | bytes 1540
  152.2 4.8 %copy-start.29 = (bf16[8,32,768]{2,1,0:T(8,128)(2,1)S(1)}, bf16[8,32,768]{2,1,0:T(8,128)(2,1)}, u32[]{:S(2)}) copy-start(bf16[8,32,768]{2,1,0:T(8,128)(2,1)} %get-tuple-element.25) | copy-start | bytes 1179652
  152.2 4.8 %copy-start.43 = (s32[128]{0:T(128)S(1)}, s32[128]{0:T(128)}, u32[]{:S(2)}) copy-start(s32[128]{0:T(128)} %copy-done.42) | copy-start | bytes 1540
  152.2 5.2 %copy-start.40 = (f32[128]{0:T(128)S(1)}, f32[128]{0:T(128)}, u32[]{:S(2)}) copy-start(f32[128]{0:T(128)} %copy-done.39) | copy-start | bytes 1540
  152.2 5.2 %copy-start.48 = (s32[1,128]{1,0:T(1,128)S(1)}, s32[1,128]{1,0:T(1,128)}, u32[]{:S(2)}) copy-start(s32[1,128]{1,0:T(1,128)} %param.26) | copy-start | bytes 1540
  155.5 2.2 copy-start.30
  155.5 2.2 copy-start.55
  155.5 113.5 %collective-permute-start = (bf16[2,768,768]{2,1,0:T(8,128)(2,1)}, bf16[2,768,768]{2,1,0:T(8,128)(2,1)}, u32[]{:S(2)}, u32[]{:S(2)}) collective-permute-start(bf16[2,768,768]{2,1,0:T(8,128)(2,1)} %dynamic-slice_bitcast_fusion), channel_id=1, source_target_pairs={{0,16},{16,0},{1,17},{17,1},{2,18},{18,2},{3,19},{19,3},{4,20},{20... | collective-permute-start | bytes 7077896 | tf_op jit(solution)/shard_map/ppermute | solution.py:485
  157.0 1.6 copy-start.57
  160.9 5.6 %copy-start.7 = (f32[12,128,256]{2,1,0:T(8,128)S(1)}, f32[12,128,256]{2,1,0:T(8,128)}, u32[]{:S(2)}) copy-start(f32[12,128,256]{2,1,0:T(8,128)} %get-tuple-element.81) | copy-start | bytes 4718596
  170.3 2.1 copy-start.12
  170.7 4.7 %copy-start.19 = (bf16[12,64,128]{2,1,0:T(8,128)(2,1)}, bf16[12,64,128]{2,1,0:T(8,128)(2,1)S(1)}, u32[]{:S(2)}) copy-start(bf16[12,64,128]{2,1,0:T(8,128)(2,1)S(1)} %convolution_convert_fusion.10) | copy-start | bytes 589828
  185.0 2.3 copy-start.31
  185.0 2.3 copy-start.34
  185.0 3.0 %copy-start.26 = (bf16[12,64,128]{2,1,0:T(8,128)(2,1)S(1)}, bf16[12,64,128]{2,1,0:T(8,128)(2,1)}, u32[]{:S(2)}) copy-start(bf16[12,64,128]{2,1,0:T(8,128)(2,1)} %copy-done.25) | copy-start | bytes 589828
  186.6 1.9 copy-start.24
  261.1 7.0 %copy-start.27 = (bf16[128,768]{1,0:T(8,128)(2,1)S(1)}, bf16[128,768]{1,0:T(8,128)(2,1)}, u32[]{:S(2)}) copy-start(bf16[128,768]{1,0:T(8,128)(2,1)} %get-tuple-element.27) | copy-start | bytes 589828
  (31 other events, 33.9 us)

commit v2 on v1

--- a/solution.py
+++ b/solution.py
@@ -39,13 +39,15 @@
     pl.semaphore_wait(barrier, len(targets))
 
 
-def gather_orders(bits):
-    far = list(range(1, bits - 1))
-    near = bits - 1
-    return [far + [near, 0, bits], [0, near] + far + [bits]]
-
-
-def gather_kernel(bits, cuts, pack_ref, tok_ref, table_ref, out_ref, toks_ref, tables_ref, local_sem, send_sem, recv_sem, tok_sem):
+def gather_plan(rows, bits):
+    far, near = list(range(1, bits - 1)), bits - 1
+    orders = [far + [near, 0, bits], far + [0, near, bits]]
+    size = 32 if rows > 64 else rows
+    starts = range(0, rows, size)
+    return [(start, min(size, rows - start), orders[n % 2]) for n, start in enumerate(starts)]
+
+
+def gather_kernel(bits, plan, pack_ref, tok_ref, table_ref, out_ref, toks_ref, tables_ref, local_sem, send_sem, recv_sem, tok_sem):
     coords = coordinates(bits)
     dims = bits + 1
     greet([partner(d, bits) for d in range(dims)])
@@ -62,13 +64,12 @@
         extras += [copy, keep]
     own = pltpu.make_async_copy(pack_ref, out_ref.at[tuple(coords)], local_sem)
     own.start()
-    orders = gather_orders(bits)
-    done = [[] for _ in cuts]
-    flying = [None for _ in cuts]
+    done = [[] for _ in plan]
+    flying = [None for _ in plan]
     sent = []
     for step in range(dims):
-        for part, (start, rows) in enumerate(cuts):
-            dim = orders[part][step]
+        for part, (start, rows, order) in enumerate(plan):
+            dim = order[step]
             if step == 0:
                 src = pack_ref.at[pl.ds(start, rows)]
                 dst = out_ref.at[tuple(coords) + (pl.ds(start, rows),)]
@@ -101,11 +102,11 @@
 
 def gather_all(pack, tokens, table, bits):
     rows, columns = pack.shape
-    cuts = [(0, 48), (48, rows - 48)] if rows > 64 else [(0, rows)]
+    plan = gather_plan(rows, bits)
     lead = (2,) * (bits + 1)
     any_spec = pl.BlockSpec(memory_space=pl.ANY)
     return pl.pallas_call(
-        functools.partial(gather_kernel, bits, cuts),
+        functools.partial(gather_kernel, bits, plan),
         out_shape=(
             jax.ShapeDtypeStruct(lead + (rows, columns), BF16),
             jax.ShapeDtypeStruct((2,) + tokens.shape, BF16),
@@ -115,19 +116,17 @@
         out_specs=(any_spec,) * 3,
         scratch_shapes=[
             pltpu.SemaphoreType.DMA,
-            pltpu.SemaphoreType.DMA((len(cuts), bits + 1)),
-            pltpu.SemaphoreType.DMA((len(cuts), bits + 1)),
+            pltpu.SemaphoreType.DMA((len(plan), bits + 1)),
+            pltpu.SemaphoreType.DMA((len(plan), bits + 1)),
             pltpu.SemaphoreType.DMA((3, 2)),
         ],
         compiler_params=pltpu.CompilerParams(collective_id=0, has_side_effects=True, vmem_limit_bytes=VMEM_LIMIT),
     )(pack, tokens, table)
 
 
-def reduce_kernel(bits, parts, *refs):
-    ins, table_ref, far_ref = refs[:parts], refs[parts], refs[parts + 1]
-    outs, table_out, far_out = refs[parts + 2 : 2 * parts + 2], refs[2 * parts + 2], refs[2 * parts + 3]
-    rest = list(refs[2 * parts + 4 :])
-    dims = bits + 1
+def reduce_kernel(bits, plan, in_ref, table_ref, far_ref, out_ref, table_out, far_out, *rest):
+    parts, dims = len(plan), bits + 1
+    rest = list(rest)
     landed = [rest[p * dims : (p + 1) * dims] for p in range(parts)]
     rest = rest[parts * dims :]
     sums = [rest[p * bits : (p + 1) * bits] for p in range(parts)]
@@ -139,8 +138,8 @@
         far_ref, far_out, far_sem.at[0], far_sem.at[1], device_id=partner(0, bits), device_id_type=MESH
     )
     far_copy.start()
-    orders = [list(reversed(order)) for order in gather_orders(bits)]
-    held = list(ins)
+    orders = [list(reversed(order)) for _, _, order in plan]
+    held = [in_ref.at[(slice(None),) * dims + (pl.ds(start, rows),)] for start, rows, _ in plan]
     left = [list(range(dims)) for _ in range(parts)]
     sent = [far_copy]
     table_now = table_ref
@@ -176,7 +175,7 @@
             total = held[part][whole + (coords[dim],)].astype(F32) + landed[part][step][...].astype(F32)
             left[part].remove(dim)
             if step == dims - 1:
-                outs[part][...] = total
+                out_ref[pl.ds(plan[part][0], plan[part][1])] = total
             else:
                 sums[part][step][...] = total.astype(BF16)
                 held[part] = sums[part][step]
@@ -192,15 +191,17 @@
         copy.wait_send()
 
 
-def reduce_all(parts, table, far, bits):
+def reduce_all(blocks, table, far, bits):
     dims = bits + 1
+    rows, width = blocks.shape[-2:]
+    plan = gather_plan(rows, bits)
     vmem = pl.BlockSpec(memory_space=pltpu.VMEM)
-    count = len(parts)
+    count = len(plan)
     scratch = []
-    for part in parts:
-        scratch += [pltpu.VMEM((2,) * (dims - 1 - s) + part.shape[-2:], BF16) for s in range(dims)]
-    for part in parts:
-        scratch += [pltpu.VMEM((2,) * (dims - 1 - s) + part.shape[-2:], BF16) for s in range(dims - 1)]
+    for _, part_rows, _ in plan:
+        scratch += [pltpu.VMEM((2,) * (dims - 1 - s) + (part_rows, width), BF16) for s in range(dims)]
+    for _, part_rows, _ in plan:
+        scratch += [pltpu.VMEM((2,) * (dims - 1 - s) + (part_rows, width), BF16) for s in range(dims - 1)]
     scratch += [
         pltpu.VMEM((dims,) + table.shape, F32),
         pltpu.VMEM((dims,) + table.shape, F32),
@@ -210,14 +211,17 @@
         pltpu.SemaphoreType.DMA((2,)),
     ]
     return pl.pallas_call(
-        functools.partial(reduce_kernel, bits, count),
-        out_shape=tuple(jax.ShapeDtypeStruct(part.shape[-2:], F32) for part in parts)
-        + (jax.ShapeDtypeStruct(table.shape, F32), jax.ShapeDtypeStruct(far.shape, BF16)),
-        in_specs=[vmem] * (count + 2),
-        out_specs=(vmem,) * (count + 2),
+        functools.partial(reduce_kernel, bits, plan),
+        out_shape=(
+            jax.ShapeDtypeStruct((rows, width), F32),
+            jax.ShapeDtypeStruct(table.shape, F32),
+            jax.ShapeDtypeStruct(far.shape, BF16),
+        ),
+        in_specs=[vmem] * 3,
+        out_specs=(vmem,) * 3,
         scratch_shapes=scratch,
         compiler_params=pltpu.CompilerParams(collective_id=1, has_side_effects=True, vmem_limit_bytes=VMEM_LIMIT),
-    )(*parts, table, far)
+    )(blocks, table, far)
 
 
 def contract(a, b, on_a, on_b):
@@ -228,62 +232,63 @@
 
 
 def expert_kernel(
-    chips, buf_ref, grad_ref, w_in_ref, w_out_ref, slots_ref, gslots_ref, wgrad_ref,
-    rows_x, rows_g, act_ref, gpre_ref, part_ref, sib_ref, ret_ref,
+    chips, both_ref, w_in_ref, w_out_ref, back_ref, keep_ref, leave_ref,
+    rows_ref, x_ref, g_ref, act_ref, gpre_ref, part_ref, sib_ref, ret_ref,
     in_sem, fwd_sem, sib_sem, out_sem,
 ):
     seq, shard = lax.axis_index("seq"), lax.axis_index("shard")
     chip, core = shard // 2, shard % 2
     sibling = (seq, shard + 1 - 2 * core)
-    capacity, width = buf_ref.shape[1:]
+    slots, width = both_ref.shape[1] // 2, both_ref.shape[2]
     hidden = w_in_ref.shape[1]
 
     def device_of(other):
         return (seq, 2 * other + core)
 
     greet([device_of((chip + j) % chips) for j in range(1, chips)] + [sibling])
-    pairs = ((buf_ref, rows_x), (grad_ref, rows_g))
     sent = []
     copies = {}
     for j in range(1, chips):
         to = (chip + j) % chips
-        for n, (src, dst) in enumerate(pairs):
-            copy = pltpu.make_async_remote_copy(
-                src.at[to], dst.at[chip, core], in_sem.at[0, n, j], in_sem.at[1, n, j],
-                device_id=device_of(to), device_id_type=MESH,
-            )
-            copy.start()
-            copies[n, j] = copy
-            sent.append(copy)
-    for n, (src, dst) in enumerate(pairs):
-        dst[chip, core] = src[chip]
+        copy = pltpu.make_async_remote_copy(
+            both_ref.at[to], rows_ref.at[chip, core], in_sem.at[0, j], in_sem.at[1, j],
+            device_id=device_of(to), device_id_type=MESH,
+        )
+        copy.start()
+        copies[j] = copy
+        sent.append(copy)
+    rows_ref[chip, core] = both_ref[chip]
     forwards = []
     for j in range(chips):
         source = (chip + chips - j) % chips
-        for n, (src, dst) in enumerate(pairs):
-            if j:
-                copies[n, j].wait_recv()
-            copy = pltpu.make_async_remote_copy(
-                dst.at[source, core], dst.at[source, core], fwd_sem.at[0, n, j], fwd_sem.at[1, n, j],
-                device_id=sibling, device_id_type=MESH,
-            )
-            copy.start()
-            forwards.append(copy)
-            sent.append(copy)
+        if j:
+            copies[j].wait_recv()
+        copy = pltpu.make_async_remote_copy(
+            rows_ref.at[source, core], rows_ref.at[source, core], fwd_sem.at[0, j], fwd_sem.at[1, j],
+            device_id=sibling, device_id_type=MESH,
+        )
+        copy.start()
+        forwards.append(copy)
+        sent.append(copy)
     for copy in forwards:
         copy.wait_recv()
 
-    group = max(1, 256 // (2 * capacity))
-    block = group * 2 * capacity
+    group = chips
+    while group * 2 * slots > 512:
+        group //= 2
+    block = group * 2 * slots
     piece = 512
 
     @pl.loop(0, chips // group)
     def _(t):
-        x = rows_x[pl.ds(t * group, group)].reshape(block, width)
-        g = rows_g[pl.ds(t * group, group)].reshape(block, width)
+        rows = rows_ref[pl.ds(t * group, group)].astype(F32)
+        x = rows[:, :, :slots].reshape(block, width).astype(BF16)
+        g = rows[:, :, slots:].reshape(block, width).astype(BF16)
         out_sum = jnp.zeros((block, width), F32)
         half_sum = jnp.zeros((block, width), F32)
         where = pl.ds(pl.multiple_of(t * block, block), block)
+        x_ref[where] = x
+        g_ref[where] = g
         for h in range(hidden // piece):
             cols = pl.ds(h * piece, piece)
             pre = jnp.dot(x, w_in_ref[:, cols], preferred_element_type=F32)
@@ -299,78 +304,69 @@
             gpre_ref[where, cols] = gpre
             out_sum += jnp.dot(act, w_out_ref[cols, :], preferred_element_type=F32)
             half_sum += contract(gpre, w_in_ref[:, cols], 1, 1)
-        out_b = out_sum.astype(BF16).reshape(group, 2, capacity, width)
-        half_b = half_sum.astype(BF16).reshape(group, 2, capacity, width)
+        out_sum = out_sum.reshape(group, 2, slots, width)
+        half_sum = half_sum.reshape(group, 2, slots, width)
+        both = jnp.concatenate([out_sum, half_sum], axis=2).astype(BF16)
         for u in range(2):
-            part_ref[0, u, pl.ds(t * group, group)] = out_b[:, u]
-            part_ref[1, u, pl.ds(t * group, group)] = half_b[:, u]
-
-    swaps = []
-    for n in range(2):
+            part_ref[u, pl.ds(t * group, group)] = both[:, u]
+
+    swap = pltpu.make_async_remote_copy(
+        part_ref.at[1 - core], sib_ref, sib_sem.at[0], sib_sem.at[1], device_id=sibling, device_id_type=MESH
+    )
+    swap.start()
+    sent.append(swap)
+    side = hidden // 2
+    away = pl.ds(pl.multiple_of((1 - seq) * side, side), side)
+    home = pl.ds(pl.multiple_of(seq * side, side), side)
+    returns = []
+    swap.wait_recv()
+    ret_ref[...] = (part_ref[core].astype(F32) + sib_ref[...].astype(F32)).astype(BF16)
+    for j in range(1, chips):
+        to = (chip + j) % chips
         copy = pltpu.make_async_remote_copy(
-            part_ref.at[n, 1 - core], sib_ref.at[n], sib_sem.at[0, n], sib_sem.at[1, n],
-            device_id=sibling, device_id_type=MESH,
+            ret_ref.at[to], back_ref.at[chip], out_sem.at[0, j], out_sem.at[1, j],
+            device_id=device_of(to), device_id_type=MESH,
         )
         copy.start()
-        swaps.append(copy)
+        returns.append(copy)
         sent.append(copy)
-    returns = []
-    outs = (slots_ref, gslots_ref)
-    for n in range(2):
-        swaps[n].wait_recv()
-        ret_ref[n] = (part_ref[n, core].astype(F32) + sib_ref[n].astype(F32)).astype(BF16)
-        for j in range(1, chips):
-            to = (chip + j) % chips
-            copy = pltpu.make_async_remote_copy(
-                ret_ref.at[n, to], outs[n].at[chip], out_sem.at[0, n, j], out_sem.at[1, n, j],
-                device_id=device_of(to), device_id_type=MESH,
-            )
-            copy.start()
-            returns.append(copy)
-            sent.append(copy)
-        outs[n][chip] = ret_ref[n, chip]
-    all_x = rows_x[...].reshape(-1, width)
-    all_g = rows_g[...].reshape(-1, width)
-    side = hidden // 2
-    for h in range(2):
-        cols = pl.ds(h * side, side)
-        wgrad_ref[h, 0] = contract(all_x, gpre_ref[:, cols], 0, 0).astype(BF16)
-        wgrad_ref[h, 1] = contract(act_ref[:, cols], all_g, 0, 0).astype(BF16)
+    back_ref[chip] = ret_ref[chip]
+    for target, cols in ((leave_ref, away), (keep_ref, home)):
+        target[0] = contract(x_ref[...], gpre_ref[:, cols], 0, 0).astype(BF16)
+        target[1] = contract(act_ref[:, cols], g_ref[...], 0, 0).astype(BF16)
     for copy in returns:
         copy.wait_recv()
     for copy in sent:
         copy.wait_send()
 
 
-def run_experts(buffer, grad_slots, w_in, w_out):
-    chips, capacity, width = buffer.shape
+def run_experts(both, w_in, w_out):
+    chips, doubled, width = both.shape
     hidden = w_in.shape[1]
-    rows = chips * 2 * capacity
+    rows = chips * doubled
     vmem = pl.BlockSpec(memory_space=pltpu.VMEM)
+    half = jax.ShapeDtypeStruct((2, width, hidden // 2), BF16)
     return pl.pallas_call(
         functools.partial(expert_kernel, chips),
-        out_shape=(
-            jax.ShapeDtypeStruct(buffer.shape, BF16),
-            jax.ShapeDtypeStruct(buffer.shape, BF16),
-            jax.ShapeDtypeStruct((2, 2, width, hidden // 2), BF16),
-        ),
-        in_specs=[vmem] * 4,
+        out_shape=(jax.ShapeDtypeStruct(both.shape, BF16), half, half),
+        in_specs=[vmem] * 3,
         out_specs=(vmem,) * 3,
         scratch_shapes=[
-            pltpu.VMEM((chips, 2, capacity, width), BF16),
-            pltpu.VMEM((chips, 2, capacity, width), BF16),
+            pltpu.VMEM((chips, 2, doubled, width), BF16),
+            pltpu.VMEM((rows, width), BF16),
+            pltpu.VMEM((rows, width), BF16),
             pltpu.VMEM((rows, hidden), BF16),
             pltpu.VMEM((rows, hidden), BF16),
-            pltpu.VMEM((2, 2, chips, capacity, width), BF16),
-            pltpu.VMEM((2, chips, capacity, width), BF16),
-            pltpu.VMEM((2, chips, capacity, width), BF16),
-            pltpu.SemaphoreType.DMA((2, 2, chips)),
-            pltpu.SemaphoreType.DMA((2, 2, chips)),
-            pltpu.SemaphoreType.DMA((2, 2)),
-            pltpu.SemaphoreType.DMA((2, 2, chips)),
+            pltpu.VMEM((2, chips, doubled, width), BF16),
+            pltpu.VMEM((chips, doubled, width), BF16),
+            pltpu.VMEM((chips, doubled, width), BF16),
+            pltpu.SemaphoreType.DMA((2, chips)),
+            pltpu.SemaphoreType.DMA((2, chips)),
+            pltpu.SemaphoreType.DMA((2,)),
+            pltpu.SemaphoreType.DMA((2, chips)),
         ],
         compiler_params=pltpu.CompilerParams(collective_id=2, has_side_effects=True, vmem_limit_bytes=VMEM_LIMIT),
-    )(buffer, grad_slots, w_in, w_out)
+    )(both, w_in, w_out)
 
 
 def rms_parts(values):
@@ -415,7 +411,7 @@
     tokens_here = tokens_in.shape[1]
     length = 2 * tokens_here
     capacity = 2 * max(1, 5 * tokens_here // (8 * experts))
-    slots = round_up(capacity, 16)
+    slots = round_up(capacity, 8)
     pack_rows = round_up(4 * rows + 1, 16)
     heads_side, buckets = bias_table.shape
 
@@ -475,14 +471,12 @@
     scaled = (picked * grad_out).astype(BF16)
     buffer = contract(dispatch, hidden_moe, 0, 0).astype(BF16)
     grad_slots = contract(dispatch, scaled, 0, 0).astype(BF16)
-    expert_slots, grad_buffer, expert_grads = run_experts(
-        buffer.reshape(experts, slots, width),
-        grad_slots.reshape(experts, slots, width),
-        w_expert_in[0],
-        w_expert_out[0],
-    )
-    leaving = lax.dynamic_index_in_dim(expert_grads, 1 - seq, 0, keepdims=False)
+    both = jnp.concatenate(
+        [buffer.reshape(experts, slots, width), grad_slots.reshape(experts, slots, width)], axis=1
+    )
+    returned, kept, leaving = run_experts(both, w_expert_in[0], w_expert_out[0])
     arriving = lax.ppermute(leaving, "seq", [(0, 1), (1, 0)])
+    expert_slots, grad_buffer = returned[:, :slots], returned[:, slots:]
 
     combined = jnp.dot(dispatch, expert_slots.reshape(-1, width), preferred_element_type=F32)
     block_out = after_attn + picked * combined
@@ -540,21 +534,14 @@
         by_device(grad_output),
         extra,
     ]
-    lead = (2,) * (bits + 1)
-
-    def joined(some):
-        part = jnp.concatenate(some, axis=1)
-        part = jnp.pad(part, ((0, 0), (0, round_up(part.shape[1], 16) - part.shape[1]), (0, 0)))
-        return part.reshape(lead + part.shape[1:])
-
-    parts = [joined(pieces[:2]), joined(pieces[2:])] if rows % 8 == 0 else [joined(pieces)]
-    *sums, table_sum, far_sum = reduce_all(parts, grad_table, far, bits)
-    total = jnp.concatenate([sums[0][: 2 * rows], *sums[1:]], axis=0) if len(sums) > 1 else sums[0]
+    blocks = jnp.concatenate(pieces, axis=1)
+    blocks = jnp.pad(blocks, ((0, 0), (0, pack_rows - blocks.shape[1]), (0, 0)))
+    blocks = blocks.reshape((2,) * (bits + 1) + blocks.shape[1:])
+    total, table_sum, far_sum = reduce_all(blocks, grad_table, far, bits)
     share = total[4 * rows]
 
     grad_hidden_attn = back_query + mine(back_all) + far_sum.astype(F32)
     grad_tokens = grad_mid + rms_back(grad_hidden_attn * full_gain_attn, normed_attn, inverse_attn)
-    kept = lax.dynamic_index_in_dim(expert_grads, seq, 0, keepdims=False)
     expert_sum = kept.astype(F32) + arriving.astype(F32)
     return (
         block_out.astype(BF16)[None],

time: 275 us -> 251 us (0.913)
  Pallas kernels: 182 us -> 153 us
  local copies, waits for them, and re-layouts: 47.4 us -> 51.7 us
    pallas_call x2, Pallas kernels: 132 us -> 115 us  [the longest x1 63.4 us: reduce_all(): pl.pallas_call(functools.partial(reduce_kernel, bits, plan), out_shape=(j...]
    pallas_call x1, Pallas kernels: 50 us -> 38.3 us  [run_experts(): pl.pallas_call(functools.partial(expert_kernel, chips), out_shape=(jax.Sh...]
    pad x0 -> x1, local copies, waits for them, and re-layouts: none -> 5.21 us  [local(): blocks = jnp.pad(blocks, ((0, 0), (0, pack_rows - blocks.shape[1]), (0, 0)))]
    dot_general x12, matrix products: 7.53 us -> 10.9 us  [contract(): lax.dot_general(a, b, (((on_a,), (on_b,)), ((), ())), preferred_element_t...]
    squeeze x1 -> x0, local copies, waits for them, and re-layouts: 3.27 us -> none  [local(): leaving = lax.dynamic_index_in_dim(expert_grads, 1 - seq, 0, keepdims=False)]
    unnamed x134 -> x86, local copies, waits for them, and re-layouts: 12.9 us -> 9.8 us
  transfers between devices with their start and end apart: 1 -> 1, of which waited for: 0 -> 0; matrix products, arithmetic and copies ran while one was open for 14% -> 18% of each run, Pallas kernels for 26% -> 25%
where the time goes in v2:
time: 251 us; the launch traced here: 249 us
  Pallas kernels  153 us (61%)
  local copies, waits for them, and re-layouts  51.7 us (21%)
  matrix products  27.9 us (11%)
  other arithmetic  14.4 us (6%)
    pallas_call x1, Pallas kernels, reduce_all(): pl.pallas_call(functools.partial(reduce_kernel, bits, plan), out_shape=(j...  63.4 us
    pallas_call x1, Pallas kernels, gather_all(): pl.pallas_call(functools.partial(gather_kernel, bits, plan), out_shape=(j...  51.7 us
    pallas_call x1, Pallas kernels, run_experts(): pl.pallas_call(functools.partial(expert_kernel, chips), out_shape=(jax.Sh...  38.3 us
    dot_general x12, matrix products, contract(): lax.dot_general(a, b, (((on_a,), (on_b,)), ((), ())), preferred_element_t...  10.9 us
    unnamed x86, local copies, waits for them, and re-layouts  9.8 us
    pad x1, local copies, waits for them, and re-layouts, local(): blocks = jnp.pad(blocks, ((0, 0), (0, pack_rows - blocks.shape[1]), (0, 0)))  5.21 us
  transfers between devices with their start and end apart: 1, of which 0 were waited for; matrix products, arithmetic and copies ran while one was open for 18% of the time, Pallas kernels for 25%

profile of v2, /device:TPU:0, one launch (start us, length us, event | category | flops | bytes accessed | tf_op | source)
XLA Modules:
  0.0 249.4 jit_solution(13705113063736587707)
XLA Ops:
  3.3 1.3 pad.41.table_ref
  8.4 51.7 %shard_map.238 = (bf16[2,2,2,2,2,112,768]{6,5,4,3,2,1,0:T(8,128)(2,1)}, bf16[2,128,768]{2,1,0:T(8,128)(2,1)}, bf16[2,16,128]{2,1,0:T(8,128)(2,1)}) custom-call(bf16[112,768]{1,0:T(8,128)(2,1)} %pad.40.pack_ref, bf16[128,768]{1,0:T(8,128)(2,1)} %bitcast.155, bf16[16,128]{1,0:T(8,128)(2,1)} %pad.41.table_ref), custom_call_target="tpu_custom_call" | custom-call | tf_op jit(solution)/shard_map/pallas_call | solution.py:108
  61.2 3.7 %fusion.67 = (bf16[32,24,768]{2,1,0:T(8,128)(2,1)}, bf16[32,24,768]{2,1,0:T(8,128)(2,1)S(1)}, bf16[32,24,768]{2,1,0:T(8,128)(2,1)S(1)}, bf16[32,24,768]{2,1,0:T(8,128)(2,1)S(1)}) fusion(bf16[32,112,768]{2,1,0:T(8,128)(2,1)} %bitcast.157), kind=kLoop, calls=%fused_computation.135 | loop fusion | bytes 9437184 | tf_op jit(solution)/shard_map/slice | solution.py:426
  65.5 1.1 slice_convert_fusion
  66.6 1.2 multiply_reduce_fusion.2
  70.0 1.6 reshape.267
  71.6 2.0 convolution_convert_fusion.13
  73.6 1.7 copy.46
  75.3 1.2 multiply_convert_fusion.2
  79.3 1.8 copy.64
  81.3 3.4 %reshape.265 = f32[12,128,383]{2,1,0:T(8,128)} reshape(f32[12,49024]{1,0:T(8,128)S(1)} %slice.114) | data formatting | bytes 4706304 | tf_op jit(solution)/shard_map/reshape | solution.py:386
  84.7 2.4 slice_add_fusion
  87.2 1.4 fusion.71
  88.6 2.8 %convolution_convert_fusion.12 = bf16[12,64,128]{2,1,0:T(8,128)(2,1)S(1)} fusion(bf16[256,12,64]{0,2,1:T(8,128)(2,1)S(1)} %bitcast.181, f32[12,128]{1,0:T(8,128)S(1)} %get-tuple-element.80, f32[12,128,256]{2,1,0:T(8,128)S(1)} %slice_add_fusion), kind=kOutput, calls=%fused_computation.28 | convolution fusion | flops 51611392 | bytes 2168832 | tf_op jit(solution)/shard_map/hqk,khd->qhd/dot_general | solution.py:457
  94.3 38.3 %shard_map.239 = (bf16[8,48,768]{2,1,0:T(8,128)(2,1)}, bf16[2,768,768]{2,1,0:T(8,128)(2,1)}, bf16[2,768,768]{2,1,0:T(8,128)(2,1)}) custom-call(bf16[8,48,768]{2,1,0:T(8,128)(2,1)} %pad_maximum_fusion.both_ref, bf16[768,1536]{1,0:T(8,128)(2,1)} %bitcast.166, bf16[1536,768]{1,0:T(8,128)(2,1)} %bitcast.167), custom_call_target="tpu_custom_call" | custom-call | tf_op jit(solution)/shard_map/pallas_call | solution.py:349
  137.5 1.2 convolution_convert_fusion.11
  139.8 3.8 %convolution_convert_fusion.4 = bf16[12,64,256]{2,1,0:T(8,128)(2,1)} fusion(bf16[128,12,64]{0,2,1:T(8,128)(2,1)S(1)} %bitcast.184, f32[12,128]{1,0:T(8,128)S(1)} %get-tuple-element.80, f32[12,128,256]{2,1,0:T(8,128)S(1)} %slice_add_fusion), kind=kOutput, calls=%fused_computation.18 | convolution fusion | flops 51709696 | bytes 2168832 | tf_op jit(solution)/shard_map/hqk,qhd->khd/dot_general | solution.py:503
  143.6 2.3 multiply_reduce_fusion
  147.5 1.5 pad.45
  153.6 3.6 %reshape.276 = bf16[12,49024]{1,0:T(8,128)(2,1)S(1)} reshape(bf16[12,128,383]{2,1,0:T(8,128)(2,1)} %pad.45) | data formatting | bytes 2353152 | tf_op jit(solution)/shard_map/reshape | solution.py:393
  159.1 1.6 fusion.5
  160.7 1.6 fusion.4
  163.5 1.6 fusion.3
  165.1 1.5 fusion.2
  167.3 5.2 %pad.44 = bf16[32,112,768]{2,1,0:T(8,128)(2,1)} pad(bf16[32,97,768]{2,1,0:T(8,128)(2,1)} %copy_dynamic-update-slice_fusion, bf16[]{:T(256)} %constant.16.clone.1), padding=0_0x0_15x0_0 | pad | bytes 10272770 | tf_op jit(solution)/shard_map/jit(_pad)/pad | solution.py:538
  173.2 63.4 %shard_map.240 = (f32[112,768]{1,0:T(8,128)}, f32[16,128]{1,0:T(8,128)}, bf16[128,768]{1,0:T(8,128)(2,1)}) custom-call(bf16[2,2,2,2,2,112,768]{6,5,4,3,2,1,0:T(8,128)(2,1)} %bitcast.142, f32[16,128]{1,0:T(8,128)} %pad.47.table_ref, bf16[128,768]{1,0:T(8,128)(2,1)} %dynamic-slice_convert_fusion.far_ref), custom_call_target="tpu_custom_call" | custom-call | tf_op jit(solution)/shard_map/pallas_call | solution.py:213
  238.2 1.3 constant_dynamic-slice_fusion
  239.5 1.1 fusion.13
  240.6 1.4 slice_bitcast_fusion
  242.1 1.7 fusion.70
  244.7 2.2 convert_add_fusion
  246.9 2.5 fusion.68
  (153 shorter events, 35.0 us)
Async XLA Ops:
  61.2 7.2 %copy-start.35 = (bf16[2,16,128]{2,1,0:T(8,128)(2,1)S(1)}, bf16[2,16,128]{2,1,0:T(8,128)(2,1)}, u32[]{:S(2)}) copy-start(bf16[2,16,128]{2,1,0:T(8,128)(2,1)} %get-tuple-element.23) | copy-start | bytes 24580
  64.9 11.6 %copy-start.2 = (bf16[32,24,768]{2,1,0:T(8,128)(2,1)}, bf16[32,24,768]{2,1,0:T(8,128)(2,1)S(1)}, u32[]{:S(2)}) copy-start(bf16[32,24,768]{2,1,0:T(8,128)(2,1)S(1)} %get-tuple-element.58) | copy-start | bytes 3538948
  64.9 11.6 %copy-start = (bf16[32,24,768]{2,1,0:T(8,128)(2,1)}, bf16[32,24,768]{2,1,0:T(8,128)(2,1)S(1)}, u32[]{:S(2)}) copy-start(bf16[32,24,768]{2,1,0:T(8,128)(2,1)S(1)} %get-tuple-element.57) | copy-start | bytes 3538948
  64.9 12.1 %copy-start.5 = (bf16[32,24,768]{2,1,0:T(8,128)(2,1)}, bf16[32,24,768]{2,1,0:T(8,128)(2,1)S(1)}, u32[]{:S(2)}) copy-start(bf16[32,24,768]{2,1,0:T(8,128)(2,1)S(1)} %get-tuple-element.59) | copy-start | bytes 3538948
  66.6 9.8 %copy-start.32 = (f32[128]{0:T(128)}, f32[128]{0:T(128)S(1)}, u32[]{:S(2)}) copy-start(f32[128]{0:T(128)S(1)} %add_rsqrt_fusion.2) | copy-start | bytes 1540
  77.0 1.6 copy-start.36
  78.6 6.1 %copy-start.10 = (bf16[256,768]{0,1:T(8,128)(2,1)}, bf16[256,768]{0,1:T(8,128)(2,1)S(1)}, u32[]{:S(2)}) copy-start(bf16[256,768]{0,1:T(8,128)(2,1)S(1)} %copy.47) | copy-start | bytes 1179652
  87.2 1.4 copy-start.24
  88.6 2.9 %copy-start.4 = (bf16[32,24,768]{2,1,0:T(8,128)(2,1)S(1)}, bf16[32,24,768]{2,1,0:T(8,128)(2,1)}, u32[]{:S(2)}) copy-start(bf16[32,24,768]{2,1,0:T(8,128)(2,1)} %get-tuple-element.56) | copy-start | bytes 3538948
  88.6 2.9 %copy-start.7 = (bf16[1,128,768]{2,1,0:T(8,128)(2,1)S(1)}, bf16[1,128,768]{2,1,0:T(8,128)(2,1)}, u32[]{:S(2)}) copy-start(bf16[1,128,768]{2,1,0:T(8,128)(2,1)} %param.15) | copy-start | bytes 589828
  91.5 1.6 copy-start.18
  132.6 112.1 %collective-permute-start = (bf16[2,768,768]{2,1,0:T(8,128)(2,1)}, bf16[2,768,768]{2,1,0:T(8,128)(2,1)}, u32[]{:S(2)}, u32[]{:S(2)}) collective-permute-start(bf16[2,768,768]{2,1,0:T(8,128)(2,1)} %get-tuple-element.29), channel_id=1, source_target_pairs={{0,16},{16,0},{1,17},{17,1},{2,18},{18,2},{3,19},{19,3},{4,20},{20... | collective-permute-start | bytes 7077896 | tf_op jit(solution)/shard_map/ppermute | solution.py:478
  139.8 3.8 %copy-start.25 = (bf16[256,768]{0,1:T(8,128)(2,1)S(1)}, bf16[256,768]{0,1:T(8,128)(2,1)}, u32[]{:S(2)}) copy-start(bf16[256,768]{0,1:T(8,128)(2,1)} %copy.45) | copy-start | bytes 1179652
  143.6 2.3 copy-start.8
  145.8 1.4 copy-start.16
  147.2 1.8 copy-start.21
  147.2 1.8 copy-start.3
  147.5 2.1 copy-start.12
  147.5 2.1 copy-start.1
  149.6 1.3 copy-start.6
  149.6 1.3 copy-start.9
  149.6 1.4 copy-start.19
  149.6 1.4 copy-start.34
  151.1 1.5 copy-start.33
  158.1 1.0 copy-start.26
  158.1 2.6 %copy-start.13 = (bf16[12,64,256]{2,1,0:T(8,128)(2,1)S(1)}, bf16[12,64,256]{2,1,0:T(8,128)(2,1)}, u32[]{:S(2)}) copy-start(bf16[12,64,256]{2,1,0:T(8,128)(2,1)} %copy-done.12) | copy-start | bytes 1179652
  158.1 2.6 %copy-start.14 = (bf16[768,256]{1,0:T(8,128)(2,1)S(1)}, bf16[768,256]{1,0:T(8,128)(2,1)}, u32[]{:S(2)}) copy-start(bf16[768,256]{1,0:T(8,128)(2,1)} %copy.51) | copy-start | bytes 1179652
  159.1 3.2 %copy-start.27 = (bf16[768,8]{0,1:T(8,128)(2,1)S(1)}, bf16[768,8]{0,1:T(8,128)(2,1)}, u32[]{:S(2)}) copy-start(bf16[768,8]{0,1:T(8,128)(2,1)} %convolution_convert_fusion.14) | copy-start | bytes 36868
  160.7 1.9 copy-start.30
  160.7 2.8 %copy-start.20 = (bf16[12,64,256]{2,1,0:T(8,128)(2,1)S(1)}, bf16[12,64,256]{2,1,0:T(8,128)(2,1)}, u32[]{:S(2)}) copy-start(bf16[12,64,256]{2,1,0:T(8,128)(2,1)} %convolution_convert_fusion.4) | copy-start | bytes 1179652
  236.7 7.1 %copy-start.23 = (bf16[128,768]{1,0:T(8,128)(2,1)S(1)}, bf16[128,768]{1,0:T(8,128)(2,1)}, u32[]{:S(2)}) copy-start(bf16[128,768]{1,0:T(8,128)(2,1)} %get-tuple-element.25) | copy-start | bytes 589828
  240.6 4.1 %copy-start.15 = (bf16[2,768,768]{2,1,0:T(8,128)(2,1)S(1)}, bf16[2,768,768]{2,1,0:T(8,128)(2,1)}, u32[]{:S(2)}) copy-start(bf16[2,768,768]{2,1,0:T(8,128)(2,1)} %get-tuple-element.28) | copy-start | bytes 7077892
  (7 other events, 5.5 us)

commit v3 on v2

--- a/solution.py
+++ b/solution.py
@@ -124,7 +124,9 @@
     )(pack, tokens, table)
 
 
-def reduce_kernel(bits, plan, in_ref, table_ref, far_ref, out_ref, table_out, far_out, *rest):
+def reduce_kernel(bits, plan, places, inputs, *refs):
+    ins, rest = refs[:inputs], refs[inputs:]
+    table_ref, far_ref, out_ref, table_out, far_out, *rest = rest
     parts, dims = len(plan), bits + 1
     rest = list(rest)
     landed = [rest[p * dims : (p + 1) * dims] for p in range(parts)]
@@ -139,7 +141,10 @@
     )
     far_copy.start()
     orders = [list(reversed(order)) for _, _, order in plan]
-    held = [in_ref.at[(slice(None),) * dims + (pl.ds(start, rows),)] for start, rows, _ in plan]
+    held = [
+        ins[which].at[(slice(None),) * dims + (pl.ds(start, plan[part][1]),)]
+        for part, (which, start) in enumerate(places)
+    ]
     left = [list(range(dims)) for _ in range(parts)]
     sent = [far_copy]
     table_now = table_ref
@@ -193,8 +198,11 @@
 
 def reduce_all(blocks, table, far, bits):
     dims = bits + 1
-    rows, width = blocks.shape[-2:]
+    width = blocks[0].shape[-1]
+    rows = sum(block.shape[-2] for block in blocks)
     plan = gather_plan(rows, bits)
+    first = blocks[0].shape[-2]
+    places = [(0, start) if start < first else (1, start - first) for start, _, _ in plan]
     vmem = pl.BlockSpec(memory_space=pltpu.VMEM)
     count = len(plan)
     scratch = []
@@ -211,17 +219,17 @@
         pltpu.SemaphoreType.DMA((2,)),
     ]
     return pl.pallas_call(
-        functools.partial(reduce_kernel, bits, plan),
+        functools.partial(reduce_kernel, bits, plan, places, len(blocks)),
         out_shape=(
             jax.ShapeDtypeStruct((rows, width), F32),
             jax.ShapeDtypeStruct(table.shape, F32),
             jax.ShapeDtypeStruct(far.shape, BF16),
         ),
-        in_specs=[vmem] * 3,
+        in_specs=[vmem] * (len(blocks) + 2),
         out_specs=(vmem,) * 3,
         scratch_shapes=scratch,
         compiler_params=pltpu.CompilerParams(collective_id=1, has_side_effects=True, vmem_limit_bytes=VMEM_LIMIT),
-    )(blocks, table, far)
+    )(*blocks, table, far)
 
 
 def contract(a, b, on_a, on_b):
@@ -378,25 +386,118 @@
     return inverse * (grad_normed - normed * jnp.mean(grad_normed * normed, axis=-1, keepdims=True))
 
 
-def spread_offsets(per_offset, block_rows, columns):
-    heads_here = per_offset.shape[0]
-    period = block_rows + columns
-    padded = jnp.pad(per_offset, ((0, 0), (0, 1)))
-    tiled = jnp.tile(padded, (1, block_rows))[:, : block_rows * (period - 1)]
-    return tiled.reshape(heads_here, block_rows, period - 1)[:, :, block_rows - 1 :]
-
-
-def offset_sums(grid):
-    heads_here, block_rows, columns = grid.shape
-    period = block_rows + columns
-    widened = jnp.pad(grid, ((0, 0), (0, 0), (block_rows - 1, 0)))
-    flat_grid = widened.reshape(heads_here, block_rows * (period - 1))
-    flat_grid = jnp.pad(flat_grid, ((0, 0), (0, block_rows)))
-    return jnp.sum(flat_grid.reshape(heads_here, block_rows, period), axis=1)[:, : period - 1]
-
-
-def heads_of(matrix):
-    return matrix.reshape(matrix.shape[0], -1, HEAD_DIM)
+def attend_kernel(own_ref, all_ref, wq_ref, wk_ref, wv_ref, offset_ref, q_ref, k_ref, v_ref, probs_ref, mixed_ref):
+    own, every = own_ref[...], all_ref[...]
+    q_ref[...] = jnp.dot(own, wq_ref[...], preferred_element_type=F32).astype(BF16)
+    k_ref[...] = jnp.dot(every, wk_ref[...], preferred_element_type=F32).astype(BF16)
+    v_ref[...] = jnp.dot(every, wv_ref[...], preferred_element_type=F32).astype(BF16)
+    here, length = own.shape[0], every.shape[0]
+    period = offset_ref.shape[1]
+    for pair in range(probs_ref.shape[0] // 2):
+        cols = pl.ds(2 * HEAD_DIM * pair, 2 * HEAD_DIM)
+        q, k, v = q_ref[:, cols], k_ref[:, cols], v_ref[:, cols]
+        mixed = []
+        for side in range(2):
+            head = 2 * pair + side
+            part = slice(side * HEAD_DIM, (side + 1) * HEAD_DIM)
+            line = jnp.broadcast_to(offset_ref[head : head + 1, :], (here, period))
+            bias = pltpu.roll(line, period - here + 1, 1, stride=1, stride_axis=0)[:, :length]
+            scores = contract(q[:, part], k[:, part], 1, 1) + bias
+            weights = jnp.exp(scores - jnp.max(scores, axis=-1, keepdims=True))
+            probs = weights / jnp.sum(weights, axis=-1, keepdims=True)
+            probs_ref[head] = probs
+            mixed.append(jnp.dot(probs.astype(BF16), v[:, part], preferred_element_type=F32))
+        mixed_ref[:, cols] = jnp.concatenate(mixed, axis=1).astype(BF16)
+
+
+def attend(own, every, wq, wk, wv, per_offset, heads):
+    vmem = pl.BlockSpec(memory_space=pltpu.VMEM)
+    low_own = jax.ShapeDtypeStruct(own.shape, BF16)
+    low_all = jax.ShapeDtypeStruct(every.shape, BF16)
+    probs = jax.ShapeDtypeStruct((heads, own.shape[0], every.shape[0]), F32)
+    return pl.pallas_call(
+        attend_kernel,
+        out_shape=(low_own, low_all, low_all, probs, low_own),
+        in_specs=[vmem] * 6,
+        out_specs=(vmem,) * 5,
+        compiler_params=pltpu.CompilerParams(vmem_limit_bytes=VMEM_LIMIT),
+    )(own, every, wq, wk, wv, per_offset)
+
+
+def attend_back_kernel(
+    devices, own_ref, all_ref, wq_ref, wk_ref, wv_ref, wo_ref, q_ref, k_ref, v_ref, probs_ref, mixed_ref, branch_ref,
+    main_ref, back_own_ref, back_all_ref, offset_ref, gq_ref, gk_ref, gv_ref, gm_ref,
+):
+    here, length = own_ref.shape[0], all_ref.shape[0]
+    width = own_ref.shape[1]
+    period = offset_ref.shape[1]
+    branch = branch_ref[...]
+    gm_ref[...] = contract(branch, wo_ref[...], 1, 1).astype(BF16)
+    down = lax.broadcasted_iota(jnp.int32, (here, here), 0)
+    across = lax.broadcasted_iota(jnp.int32, (here, here), 1)
+    flip = jnp.where(down + across == here - 1, 1.0, 0.0).astype(BF16)
+    offset_ref[...] = jnp.zeros_like(offset_ref)
+    for pair in range(probs_ref.shape[0] // 2):
+        cols = pl.ds(2 * HEAD_DIM * pair, 2 * HEAD_DIM)
+        q, k, v, gm = q_ref[:, cols], k_ref[:, cols], v_ref[:, cols], gm_ref[:, cols]
+        grads = [[], [], []]
+        for side in range(2):
+            head = 2 * pair + side
+            part = slice(side * HEAD_DIM, (side + 1) * HEAD_DIM)
+            probs = probs_ref[head]
+            grad_probs = contract(gm[:, part], v[:, part], 1, 1)
+            centre = jnp.sum(probs * grad_probs, axis=-1, keepdims=True)
+            scores = (probs * (grad_probs - centre)).astype(BF16)
+            grads[0].append(jnp.dot(scores, k[:, part], preferred_element_type=F32))
+            grads[1].append(contract(scores, q[:, part], 0, 0))
+            grads[2].append(contract(probs.astype(BF16), gm[:, part], 0, 0))
+            turned = jnp.dot(flip, scores, preferred_element_type=F32)
+            turned = jnp.concatenate([turned, jnp.zeros((here, period - length), F32)], axis=1)
+            turned = pltpu.roll(turned, 0, 1, stride=1, stride_axis=0)
+            offset_ref[head : head + 1, :] = jnp.sum(turned, axis=0, keepdims=True)
+        for ref, halves in zip((gq_ref, gk_ref, gv_ref), grads):
+            ref[:, cols] = jnp.concatenate(halves, axis=1).astype(BF16)
+    gq, gk, gv = gq_ref[...], gk_ref[...], gv_ref[...]
+    back_own_ref[...] = contract(gq, wq_ref[...], 1, 1)
+    back_all_ref[...] = contract(gk, wk_ref[...], 1, 1) + contract(gv, wv_ref[...], 1, 1)
+    pairs = (
+        ((own_ref, gq), (all_ref, gk)),
+        ((all_ref, gv), (mixed_ref, branch)),
+    )
+    if main_ref.shape[0] == devices:
+        rows = width // devices
+        for n, some in enumerate(pairs):
+            both = [contract(left[...], right, 0, 0).reshape(devices, rows, width) for left, right in some]
+            main_ref[:, pl.ds(2 * rows * n, 2 * rows)] = jnp.concatenate(both, axis=1).astype(BF16)
+    else:
+        for n, some in enumerate(pairs):
+            for m, (left, right) in enumerate(some):
+                main_ref[2 * n + m] = contract(left[...], right, 0, 0).astype(BF16)
+
+
+def attend_back(devices, own, every, wq, wk, wv, wo, q, k, v, probs, mixed, branch, packed):
+    vmem = pl.BlockSpec(memory_space=pltpu.VMEM)
+    here, width = own.shape
+    length = every.shape[0]
+    main = (devices, 4 * (width // devices), width) if packed else (4, width, width)
+    return pl.pallas_call(
+        functools.partial(attend_back_kernel, devices),
+        out_shape=(
+            jax.ShapeDtypeStruct(main, BF16),
+            jax.ShapeDtypeStruct((here, width), F32),
+            jax.ShapeDtypeStruct((length, width), F32),
+            jax.ShapeDtypeStruct((16, here + length), F32),
+        ),
+        in_specs=[vmem] * 12,
+        out_specs=(vmem,) * 4,
+        scratch_shapes=[
+            pltpu.VMEM((here, width), BF16),
+            pltpu.VMEM((length, width), BF16),
+            pltpu.VMEM((length, width), BF16),
+            pltpu.VMEM((here, width), BF16),
+        ],
+        compiler_params=pltpu.CompilerParams(vmem_limit_bytes=VMEM_LIMIT),
+    )(own, every, wq, wk, wv, wo, q, k, v, probs, mixed, branch)
 
 
 def local(
@@ -440,22 +541,18 @@
     normed_attn, inverse_attn = rms_parts(inputs)
     hidden_all = (normed_all * full_gain_attn).astype(BF16)
     hidden_own = (normed_attn * full_gain_attn).astype(BF16)
-    queries = heads_of(jnp.dot(hidden_own, full_query, preferred_element_type=F32).astype(BF16))
-    keys = heads_of(jnp.dot(hidden_all, full_key, preferred_element_type=F32).astype(BF16))
-    values = heads_of(jnp.dot(hidden_all, full_value, preferred_element_type=F32).astype(BF16))
-
     bucket_onehot = (jnp.arange(buckets, dtype=jnp.int32)[:, None] == bucket_id[None, :]).astype(BF16)
     onehot_here = lax.dynamic_slice_in_dim(
         bucket_onehot, tokens_here * (1 - seq), tokens_here + length - 1, 1
     )
-    per_offset = jnp.dot(full_table, onehot_here, preferred_element_type=F32)
-    scores = jnp.einsum("qhd,khd->hqk", queries, keys, preferred_element_type=F32)
-    scores = scores + spread_offsets(per_offset, tokens_here, length)
-    weights = jnp.exp(scores - jnp.max(scores, axis=-1, keepdims=True))
-    probs = weights / jnp.sum(weights, axis=-1, keepdims=True)
-    probs_low = probs.astype(BF16)
-    mixed = jnp.einsum("hqk,khd->qhd", probs_low, values, preferred_element_type=F32)
-    mixed = mixed.reshape(tokens_here, width).astype(BF16)
+    onehot_here = jnp.pad(onehot_here, ((0, 0), (0, 1)))
+    heads = 2 * heads_side
+    per_offset = jnp.dot(
+        jnp.pad(full_table, ((0, 16 - heads), (0, 0))), onehot_here, preferred_element_type=F32
+    )
+    queries, keys, values, probs, mixed = attend(
+        hidden_own, hidden_all, full_query, full_key, full_value, per_offset, heads
+    )
 
     after_attn = inputs + jnp.dot(mixed, full_output, preferred_element_type=F32)
     normed_moe, inverse_moe = rms_parts(after_attn)
@@ -492,31 +589,17 @@
     grad_gain_moe = jnp.sum(grad_hidden_moe * normed_moe, axis=0)
     grad_mid = grad_out + rms_back(grad_hidden_moe * full_gain_moe, normed_moe, inverse_moe)
     grad_branch = grad_mid.astype(BF16)
-    grad_output = contract(mixed, grad_branch, 0, 0)
-    grad_mixed = heads_of(contract(grad_branch, full_output, 1, 1).astype(BF16))
-
-    grad_probs = jnp.einsum("qhd,khd->hqk", grad_mixed, values, preferred_element_type=F32)
-    centre = jnp.sum(probs * grad_probs, axis=-1, keepdims=True)
-    grad_scores = (probs * (grad_probs - centre)).astype(BF16)
-    grad_q = jnp.einsum("hqk,khd->qhd", grad_scores, keys, preferred_element_type=F32)
-    grad_k = jnp.einsum("hqk,qhd->khd", grad_scores, queries, preferred_element_type=F32)
-    grad_v = jnp.einsum("hqk,qhd->khd", probs_low, grad_mixed, preferred_element_type=F32)
-    grad_q = grad_q.reshape(tokens_here, width).astype(BF16)
-    grad_k = grad_k.reshape(length, width).astype(BF16)
-    grad_v = grad_v.reshape(length, width).astype(BF16)
-    grad_offset = offset_sums(grad_scores.astype(F32))
+    packed = rows % 8 == 0
+    main, back_query, back_all, grad_offset = attend_back(
+        devices, hidden_own, hidden_all, full_query, full_key, full_value, full_output,
+        queries, keys, values, probs, mixed, grad_branch, packed,
+    )
     grad_table = jnp.einsum(
         "ho,bo->hb", grad_offset, onehot_here.astype(F32), precision=lax.Precision.HIGHEST
     )
-    grad_table = jnp.pad(grad_table, ((0, 16 - 2 * heads_side), (0, 128 - buckets)))
-
-    back_query = contract(grad_q, full_query, 1, 1)
-    back_all = contract(grad_k, full_key, 1, 1) + contract(grad_v, full_value, 1, 1)
+    grad_table = jnp.pad(grad_table, ((0, 0), (0, 128 - buckets)))
     grad_gain_attn = jnp.sum(back_query * normed_attn, axis=0) + jnp.sum(back_all * normed_all, axis=0)
     far = lax.dynamic_slice_in_dim(back_all, (1 - seq) * tokens_here, tokens_here, 0).astype(BF16)
-
-    def by_device(matrix):
-        return matrix.reshape(devices, rows, width).astype(BF16)
 
     extra = jnp.concatenate(
         [
@@ -527,16 +610,12 @@
         axis=1,
     )
     extra = jnp.pad(extra, ((0, 0), (0, width - extra.shape[1])))[:, None].astype(BF16)
-    pieces = [
-        by_device(contract(hidden_own, grad_q, 0, 0)),
-        by_device(contract(hidden_all, grad_k, 0, 0)),
-        by_device(contract(hidden_all, grad_v, 0, 0)),
-        by_device(grad_output),
-        extra,
-    ]
-    blocks = jnp.concatenate(pieces, axis=1)
-    blocks = jnp.pad(blocks, ((0, 0), (0, pack_rows - blocks.shape[1]), (0, 0)))
-    blocks = blocks.reshape((2,) * (bits + 1) + blocks.shape[1:])
+    if packed:
+        blocks = [main, jnp.pad(extra, ((0, 0), (0, pack_rows - 4 * rows - 1), (0, 0)))]
+    else:
+        joined = jnp.concatenate([main[n].reshape(devices, rows, width) for n in range(4)] + [extra], axis=1)
+        blocks = [jnp.pad(joined, ((0, 0), (0, pack_rows - joined.shape[1]), (0, 0)))]
+    blocks = [block.reshape((2,) * (bits + 1) + block.shape[1:]) for block in blocks]
     total, table_sum, far_sum = reduce_all(blocks, grad_table, far, bits)
     share = total[4 * rows]
 

time: 251 us -> 235 us (0.936)
  Pallas kernels: 153 us -> 191 us
  local copies, waits for them, and re-layouts: 51.7 us -> 24.1 us
  matrix products: 27.9 us -> 4.48 us
    pallas_call x1 -> x3, Pallas kernels: 63.4 us -> 100 us  [the longest x1 82.6 us: reduce_all(): pl.pallas_call(functools.partial(reduce_kernel, bits, plan, places, len(b...]
    dot_general x10 -> x1, matrix products: 15 us -> 0.73 us  [local(): jnp.dot(jnp.pad(full_table, ((0, 16 - heads), (0, 0))), onehot_here, pref...]
    dot_general x12 -> x4, matrix products: 10.9 us -> 1.13 us  [contract(): lax.dot_general(a, b, (((on_a,), (on_b,)), ((), ())), preferred_element_t...]
    reshape x2 -> x0, local copies, waits for them, and re-layouts: 7.04 us -> none  [the longest x1 3.64 us: offset_sums(): flat_grid = widened.reshape(heads_here, block_rows * (period - 1))]
    pad x4 -> x2, local copies, waits for them, and re-layouts: 7.34 us -> 1.57 us  [the longest x1 0.96 us: local(): jnp.pad(extra, ((0, 0), (0, pack_rows - 4 * rows - 1), (0, 0)))]
    unnamed x86 -> x32, local copies, waits for them, and re-layouts: 9.8 us -> 4.7 us
    convert_element_type x4 -> x0, local copies, waits for them, and re-layouts: 3.91 us -> none  [the longest x1 1.74 us: local(): jnp.dot(hidden_own, full_query, preferred_element_type=F32).astype(BF16)]
  transfers between devices with their start and end apart: 1 -> 1, of which waited for: 0 -> 0; matrix products, arithmetic and copies ran while one was open for 18% -> 8% of each run, Pallas kernels for 25% -> 40%
where the time goes in v3:
time: 235 us; the launch traced here: 234 us
  Pallas kernels  191 us (81%)
  local copies, waits for them, and re-layouts  24.1 us (10%)
  other arithmetic  13.7 us (6%)
  matrix products  4.48 us (2%)
    pallas_call x1, Pallas kernels, reduce_all(): pl.pallas_call(functools.partial(reduce_kernel, bits, plan, places, len(b...  82.6 us
    pallas_call x1, Pallas kernels, gather_all(): pl.pallas_call(functools.partial(gather_kernel, bits, plan), out_shape=(j...  51.8 us
    pallas_call x1, Pallas kernels, run_experts(): pl.pallas_call(functools.partial(expert_kernel, chips), out_shape=(jax.Sh...  38.3 us
    pallas_call x1, Pallas kernels, attend_back(): pl.pallas_call(functools.partial(attend_back_kernel, devices), out_shape=...  11.9 us
    pallas_call x1, Pallas kernels, attend(): pl.pallas_call(attend_kernel, out_shape=(low_own, low_all, low_all, probs...  5.95 us
  transfers between devices with their start and end apart: 1, of which 0 were waited for; matrix products, arithmetic and copies ran while one was open for 8% of the time, Pallas kernels for 40%

profile of v3, /device:TPU:0, one launch (start us, length us, event | category | flops | bytes accessed | tf_op | source)
XLA Modules:
  0.0 234.3 jit_solution(7317216220954319564)
XLA Ops:
  0.6 0.8 constant_dynamic-update-slice_fusion.4
  1.4 0.8 copy.28
  2.3 0.8 constant_dynamic-update-slice_fusion.3
  3.1 0.8 constant_dynamic-update-slice_fusion.2
  3.8 0.8 constant_dynamic-update-slice_fusion.1
  4.6 0.7 fusion.44
  6.0 1.3 pad.35.table_ref
  7.3 1.0 fusion.11
  8.4 51.8 %shard_map.238 = (bf16[2,2,2,2,2,112,768]{6,5,4,3,2,1,0:T(8,128)(2,1)}, bf16[2,128,768]{2,1,0:T(8,128)(2,1)}, bf16[2,16,128]{2,1,0:T(8,128)(2,1)}) custom-call(bf16[112,768]{1,0:T(8,128)(2,1)} %pad.34.pack_ref, bf16[128,768]{1,0:T(8,128)(2,1)} %bitcast.79, bf16[16,128]{1,0:T(8,128)(2,1)} %pad.35.table_ref), custom_call_target="tpu_custom_call" | custom-call | tf_op jit(solution)/shard_map/pallas_call | solution.py:108
  60.2 1.1 slice.97
  61.3 4.3 %fusion.53 = (bf16[32,24,768]{2,1,0:T(8,128)(2,1)S(1)}, bf16[32,24,768]{2,1,0:T(8,128)(2,1)}, bf16[32,24,768]{2,1,0:T(8,128)(2,1)}, bf16[32,24,768]{2,1,0:T(8,128)(2,1)}) fusion(bf16[32,112,768]{2,1,0:T(8,128)(2,1)} %bitcast.82), kind=kLoop, calls=%fused_computation.100 | loop fusion | bytes 9437184 | tf_op jit(solution)/shard_map/slice | solution.py:527
  66.1 0.9 multiply_convert_fusion.all_ref
  67.0 0.8 fusion.4.own_ref
  67.8 0.7 fusion.32.offset_ref
  68.5 5.9 %shard_map.239 = (bf16[128,768]{1,0:T(8,128)(2,1)}, bf16[256,768]{1,0:T(8,128)(2,1)}, bf16[256,768]{1,0:T(8,128)(2,1)}, f32[12,128,256]{2,1,0:T(8,128)}, bf16[128,768]{1,0:T(8,128)(2,1)}) custom-call(bf16[128,768]{1,0:T(8,128)(2,1)} %fusion.4.own_ref, bf16[256,768]{1,0:T(8,128)(2,1)} %multiply_convert_fusion.all_ref, bf16[768,768]{1,0:T(8,128)(2,1)} %bitcast.77, ...), custom_call_target="tpu_custom_call" | custom-call | tf_op jit(solution)/shard_map/pallas_call | solution.py:418
  74.5 1.4 multiply_reduce_fusion.4
  77.3 0.8 pad_maximum_fusion.both_ref
  78.2 38.3 %shard_map.240 = (bf16[8,48,768]{2,1,0:T(8,128)(2,1)}, bf16[2,768,768]{2,1,0:T(8,128)(2,1)}, bf16[2,768,768]{2,1,0:T(8,128)(2,1)}) custom-call(bf16[8,48,768]{2,1,0:T(8,128)(2,1)} %pad_maximum_fusion.both_ref, bf16[768,1536]{1,0:T(8,128)(2,1)} %bitcast.84, bf16[1536,768]{1,0:T(8,128)(2,1)} %bitcast.85), custom_call_target="tpu_custom_call" | custom-call | tf_op jit(solution)/shard_map/pallas_call | solution.py:357
  117.1 1.1 fusion.55
  119.4 0.8 fusion.52.branch_ref
  120.7 11.9 %shard_map.241 = (bf16[32,96,768]{2,1,0:T(8,128)(2,1)}, f32[128,768]{1,0:T(8,128)}, f32[256,768]{1,0:T(8,128)}, f32[16,384]{1,0:T(8,128)}) custom-call(bf16[128,768]{1,0:T(8,128)(2,1)} %fusion.4.own_ref, bf16[256,768]{1,0:T(8,128)(2,1)} %multiply_convert_fusion.all_ref, bf16[768,768]{1,0:T(8,128)(2,1)} %bitcast.78, bf16[768,768]{1,0:T(8,128)(2,1)} %bitcast.76, ...), custom_call_target="tpu_custom_call" | custom-call | tf_op jit(solution)/shard_map/pallas_call | solution.py:483
  132.7 1.2 fusion.5
  133.9 1.3 multiply_reduce_fusion
  135.6 1.0 pad.39.clone
  138.0 82.6 %shard_map.242 = (f32[112,768]{1,0:T(8,128)}, f32[16,128]{1,0:T(8,128)}, bf16[128,768]{1,0:T(8,128)(2,1)}) custom-call(bf16[2,2,2,2,2,96,768]{6,5,4,3,2,1,0:T(8,128)(2,1)} %bitcast.80, bf16[2,2,2,2,2,16,768]{6,5,4,3,2,1,0:T(8,128)(2,1)} %bitcast.83, f32[16,128]{1,0:T(8,128)} %pad.40.refs_2_, bf16[128,768]{1,0:T(8,128)(2,1)} %dynamic-slice_convert_fusion.refs_3_), custom_call_target="tpu_custom_call" | custom-call | tf_op jit(solution)/shard_map/pallas_call | solution.py:221
  222.0 1.3 constant_dynamic-slice_fusion
  223.3 1.3 fusion.6
  224.6 1.3 slice_bitcast_fusion
  225.9 1.7 fusion.56
  227.6 2.0 fusion.10
  229.7 2.2 convert_add_fusion
  231.8 2.5 %fusion.54 = (f32[1,768,768]{2,1,0:T(8,128)}, f32[1,768,768]{2,1,0:T(8,128)}) fusion(f32[2,768,768]{2,1,0:T(8,128)S(1)} %convert_add_fusion), kind=kLoop, calls=%fused_computation.101 | loop fusion | bytes 9437184 | tf_op jit(solution)/shard_map/slice | solution.py:637
  (70 shorter events, 8.2 us)
Async XLA Ops:
  61.2 4.5 %copy-start.10 = (s32[511]{0:T(512)S(1)}, s32[511]{0:T(512)}, u32[]{:S(2)}) copy-start(s32[511]{0:T(512)} %param.28) | copy-start | bytes 6136
  61.2 4.5 %copy-start.9 = (bf16[2,16,128]{2,1,0:T(8,128)(2,1)S(1)}, bf16[2,16,128]{2,1,0:T(8,128)(2,1)}, u32[]{:S(2)}) copy-start(bf16[2,16,128]{2,1,0:T(8,128)(2,1)} %get-tuple-element.32) | copy-start | bytes 24580
  61.3 4.6 %copy-start.4 = (bf16[2,128,768]{2,1,0:T(8,128)(2,1)S(1)}, bf16[2,128,768]{2,1,0:T(8,128)(2,1)}, u32[]{:S(2)}) copy-start(bf16[2,128,768]{2,1,0:T(8,128)(2,1)} %get-tuple-element.31) | copy-start | bytes 1179652
  61.3 5.7 %copy-start.1 = (bf16[1,128,768]{2,1,0:T(8,128)(2,1)S(1)}, bf16[1,128,768]{2,1,0:T(8,128)(2,1)}, u32[]{:S(2)}) copy-start(bf16[1,128,768]{2,1,0:T(8,128)(2,1)} %param.15) | copy-start | bytes 589828
  65.6 8.9 %copy-start = (bf16[32,24,768]{2,1,0:T(8,128)(2,1)}, bf16[32,24,768]{2,1,0:T(8,128)(2,1)S(1)}, u32[]{:S(2)}) copy-start(bf16[32,24,768]{2,1,0:T(8,128)(2,1)S(1)} %get-tuple-element.74) | copy-start | bytes 3538948
  74.5 2.0 copy-start.8
  74.5 2.1 copy-start.11
  74.5 2.5 %copy-start.5 = (bf16[1,128,768]{2,1,0:T(8,128)(2,1)S(1)}, bf16[1,128,768]{2,1,0:T(8,128)(2,1)}, u32[]{:S(2)}) copy-start(bf16[1,128,768]{2,1,0:T(8,128)(2,1)} %param.29) | copy-start | bytes 589828
  116.5 113.2 %collective-permute-start = (bf16[2,768,768]{2,1,0:T(8,128)(2,1)}, bf16[2,768,768]{2,1,0:T(8,128)(2,1)}, u32[]{:S(2)}, u32[]{:S(2)}) collective-permute-start(bf16[2,768,768]{2,1,0:T(8,128)(2,1)} %get-tuple-element.47), channel_id=1, source_target_pairs={{0,16},{16,0},{1,17},{17,1},{2,18},{18,2},{3,19},{19,3},{4,20},{20... | collective-permute-start | bytes 7077896 | tf_op jit(solution)/shard_map/ppermute | solution.py:575
  132.6 3.9 %copy-start.7 = (f32[16,384]{1,0:T(8,128)S(1)}, f32[16,384]{1,0:T(8,128)}, u32[]{:S(2)}) copy-start(f32[16,384]{1,0:T(8,128)} %get-tuple-element.42) | copy-start | bytes 73732
  132.7 4.6 %copy-start.2 = (f32[256,768]{1,0:T(8,128)S(1)}, f32[256,768]{1,0:T(8,128)}, u32[]{:S(2)}) copy-start(f32[256,768]{1,0:T(8,128)} %get-tuple-element.40) | copy-start | bytes 2359300
  138.0 85.3 %copy-start.3 = (f32[128,768]{1,0:T(8,128)S(1)}, f32[128,768]{1,0:T(8,128)}, u32[]{:S(2)}) copy-start(f32[128,768]{1,0:T(8,128)} %get-tuple-element.39) | copy-start | bytes 1179652
  223.3 6.3 %copy-start.6 = (bf16[2,768,768]{2,1,0:T(8,128)(2,1)S(1)}, bf16[2,768,768]{2,1,0:T(8,128)(2,1)}, u32[]{:S(2)}) copy-start(bf16[2,768,768]{2,1,0:T(8,128)(2,1)} %get-tuple-element.46) | copy-start | bytes 7077892

commit v4 on v3

--- a/solution.py
+++ b/solution.py
@@ -140,7 +140,7 @@
         far_ref, far_out, far_sem.at[0], far_sem.at[1], device_id=partner(0, bits), device_id_type=MESH
     )
     far_copy.start()
-    orders = [list(reversed(order)) for _, _, order in plan]
+    order = list(range(bits, -1, -1))
     held = [
         ins[which].at[(slice(None),) * dims + (pl.ds(start, plan[part][1]),)]
         for part, (which, start) in enumerate(places)
@@ -148,23 +148,26 @@
     left = [list(range(dims)) for _ in range(parts)]
     sent = [far_copy]
     table_now = table_ref
+    flying = [None] * parts
+
+    def begin(part, step):
+        dim = order[step]
+        whole = (slice(None),) * left[part].index(dim)
+        copy = pltpu.make_async_remote_copy(
+            held[part].at[whole + (1 - coords[dim],)],
+            landed[part][step],
+            send_sem.at[part, step],
+            recv_sem.at[part, step],
+            device_id=partner(dim, bits),
+            device_id_type=MESH,
+        )
+        copy.start()
+        sent.append(copy)
+        flying[part] = (copy, whole, dim)
+
+    for part in range(parts):
+        begin(part, 0)
     for step in range(dims):
-        flying = []
-        for part in range(parts):
-            dim = orders[part][step]
-            spot = left[part].index(dim)
-            whole = (slice(None),) * spot
-            copy = pltpu.make_async_remote_copy(
-                held[part].at[whole + (1 - coords[dim],)],
-                landed[part][step],
-                send_sem.at[part, step],
-                recv_sem.at[part, step],
-                device_id=partner(dim, bits),
-                device_id_type=MESH,
-            )
-            copy.start()
-            sent.append(copy)
-            flying.append((copy, whole, dim))
         small = pltpu.make_async_remote_copy(
             table_now,
             table_landed.at[step],
@@ -175,7 +178,8 @@
         )
         small.start()
         sent.append(small)
-        for part, (copy, whole, dim) in enumerate(flying):
+        for part in range(parts):
+            copy, whole, dim = flying[part]
             copy.wait_recv()
             total = held[part][whole + (coords[dim],)].astype(F32) + landed[part][step][...].astype(F32)
             left[part].remove(dim)
@@ -184,6 +188,7 @@
             else:
                 sums[part][step][...] = total.astype(BF16)
                 held[part] = sums[part][step]
+                begin(part, step + 1)
         small.wait_recv()
         total = table_now[...] + table_landed[step]
         if step == dims - 1:

time: 235 us -> 222 us (0.945)
  Pallas kernels: 191 us -> 178 us
    pallas_call x1, Pallas kernels: 82.6 us -> 69.9 us  [reduce_all(): pl.pallas_call(functools.partial(reduce_kernel, bits, plan, places, len(b...]
  transfers between devices with their start and end apart: 1 -> 1, of which waited for: 0 -> 0; matrix products, arithmetic and copies ran while one was open for 8% -> 8% of each run, Pallas kernels for 40% -> 37%
where the time goes in v4:
time: 222 us
  Pallas kernels  178 us (80%)
  local copies, waits for them, and re-layouts  24.1 us (11%)
  other arithmetic  13.7 us (6%)
  matrix products  4.48 us (2%)
    pallas_call x1, Pallas kernels, reduce_all(): pl.pallas_call(functools.partial(reduce_kernel, bits, plan, places, len(b...  69.9 us
    pallas_call x1, Pallas kernels, gather_all(): pl.pallas_call(functools.partial(gather_kernel, bits, plan), out_shape=(j...  51.8 us
    pallas_call x1, Pallas kernels, run_experts(): pl.pallas_call(functools.partial(expert_kernel, chips), out_shape=(jax.Sh...  38.3 us
    pallas_call x1, Pallas kernels, attend_back(): pl.pallas_call(functools.partial(attend_back_kernel, devices), out_shape=...  11.9 us
    pallas_call x1, Pallas kernels, attend(): pl.pallas_call(attend_kernel, out_shape=(low_own, low_all, low_all, probs...  5.95 us
    unnamed x32, local copies, waits for them, and re-layouts  4.7 us
  transfers between devices with their start and end apart: 1, of which 0 were waited for; matrix products, arithmetic and copies ran while one was open for 8% of the time, Pallas kernels for 37%

profile of v4, /device:TPU:0, one launch (start us, length us, event | category | flops | bytes accessed | tf_op | source)
XLA Modules:
  0.0 221.7 jit_solution(13871443676369586672)
XLA Ops:
  0.6 0.8 constant_dynamic-update-slice_fusion.4
  1.4 0.8 copy.28
  2.3 0.8 constant_dynamic-update-slice_fusion.3
  3.1 0.8 constant_dynamic-update-slice_fusion.2
  3.8 0.8 constant_dynamic-update-slice_fusion.1
  4.6 0.7 fusion.44
  6.0 1.3 pad.35.table_ref
  7.3 1.0 fusion.11
  8.4 51.8 %shard_map.238 = (bf16[2,2,2,2,2,112,768]{6,5,4,3,2,1,0:T(8,128)(2,1)}, bf16[2,128,768]{2,1,0:T(8,128)(2,1)}, bf16[2,16,128]{2,1,0:T(8,128)(2,1)}) custom-call(bf16[112,768]{1,0:T(8,128)(2,1)} %pad.34.pack_ref, bf16[128,768]{1,0:T(8,128)(2,1)} %bitcast.79, bf16[16,128]{1,0:T(8,128)(2,1)} %pad.35.table_ref), custom_call_target="tpu_custom_call" | custom-call | tf_op jit(solution)/shard_map/pallas_call | solution.py:108
  60.2 1.1 slice.97
  61.3 4.3 %fusion.53 = (bf16[32,24,768]{2,1,0:T(8,128)(2,1)S(1)}, bf16[32,24,768]{2,1,0:T(8,128)(2,1)}, bf16[32,24,768]{2,1,0:T(8,128)(2,1)}, bf16[32,24,768]{2,1,0:T(8,128)(2,1)}) fusion(bf16[32,112,768]{2,1,0:T(8,128)(2,1)} %bitcast.82), kind=kLoop, calls=%fused_computation.100 | loop fusion | bytes 9437184 | tf_op jit(solution)/shard_map/slice | solution.py:532
  66.1 0.9 multiply_convert_fusion.all_ref
  67.0 0.8 fusion.4.own_ref
  67.8 0.7 fusion.32.offset_ref
  68.5 5.9 %shard_map.239 = (bf16[128,768]{1,0:T(8,128)(2,1)}, bf16[256,768]{1,0:T(8,128)(2,1)}, bf16[256,768]{1,0:T(8,128)(2,1)}, f32[12,128,256]{2,1,0:T(8,128)}, bf16[128,768]{1,0:T(8,128)(2,1)}) custom-call(bf16[128,768]{1,0:T(8,128)(2,1)} %fusion.4.own_ref, bf16[256,768]{1,0:T(8,128)(2,1)} %multiply_convert_fusion.all_ref, bf16[768,768]{1,0:T(8,128)(2,1)} %bitcast.77, ...), custom_call_target="tpu_custom_call" | custom-call | tf_op jit(solution)/shard_map/pallas_call | solution.py:423
  74.5 1.4 multiply_reduce_fusion.4
  77.3 0.8 pad_maximum_fusion.both_ref
  78.2 38.3 %shard_map.240 = (bf16[8,48,768]{2,1,0:T(8,128)(2,1)}, bf16[2,768,768]{2,1,0:T(8,128)(2,1)}, bf16[2,768,768]{2,1,0:T(8,128)(2,1)}) custom-call(bf16[8,48,768]{2,1,0:T(8,128)(2,1)} %pad_maximum_fusion.both_ref, bf16[768,1536]{1,0:T(8,128)(2,1)} %bitcast.84, bf16[1536,768]{1,0:T(8,128)(2,1)} %bitcast.85), custom_call_target="tpu_custom_call" | custom-call | tf_op jit(solution)/shard_map/pallas_call | solution.py:362
  117.1 1.1 fusion.55
  119.4 0.8 fusion.52.branch_ref
  120.7 11.9 %shard_map.241 = (bf16[32,96,768]{2,1,0:T(8,128)(2,1)}, f32[128,768]{1,0:T(8,128)}, f32[256,768]{1,0:T(8,128)}, f32[16,384]{1,0:T(8,128)}) custom-call(bf16[128,768]{1,0:T(8,128)(2,1)} %fusion.4.own_ref, bf16[256,768]{1,0:T(8,128)(2,1)} %multiply_convert_fusion.all_ref, bf16[768,768]{1,0:T(8,128)(2,1)} %bitcast.78, bf16[768,768]{1,0:T(8,128)(2,1)} %bitcast.76, ...), custom_call_target="tpu_custom_call" | custom-call | tf_op jit(solution)/shard_map/pallas_call | solution.py:488
  132.7 1.2 fusion.5
  133.9 1.3 multiply_reduce_fusion
  135.6 1.0 pad.39.clone
  138.0 69.9 %shard_map.242 = (f32[112,768]{1,0:T(8,128)}, f32[16,128]{1,0:T(8,128)}, bf16[128,768]{1,0:T(8,128)(2,1)}) custom-call(bf16[2,2,2,2,2,96,768]{6,5,4,3,2,1,0:T(8,128)(2,1)} %bitcast.80, bf16[2,2,2,2,2,16,768]{6,5,4,3,2,1,0:T(8,128)(2,1)} %bitcast.83, f32[16,128]{1,0:T(8,128)} %pad.40.refs_2_, bf16[128,768]{1,0:T(8,128)(2,1)} %dynamic-slice_convert_fusion.refs_3_), custom_call_target="tpu_custom_call" | custom-call | tf_op jit(solution)/shard_map/pallas_call | solution.py:226
  209.3 1.3 constant_dynamic-slice_fusion
  210.6 1.3 fusion.6
  211.9 1.3 slice_bitcast_fusion
  213.3 1.7 fusion.56
  215.0 2.0 fusion.10
  217.0 2.2 convert_add_fusion
  219.2 2.5 %fusion.54 = (f32[1,768,768]{2,1,0:T(8,128)}, f32[1,768,768]{2,1,0:T(8,128)}) fusion(f32[2,768,768]{2,1,0:T(8,128)S(1)} %convert_add_fusion), kind=kLoop, calls=%fused_computation.101 | loop fusion | bytes 9437184 | tf_op jit(solution)/shard_map/slice | solution.py:642
  (70 shorter events, 8.2 us)
Async XLA Ops:
  61.2 4.5 %copy-start.10 = (s32[511]{0:T(512)S(1)}, s32[511]{0:T(512)}, u32[]{:S(2)}) copy-start(s32[511]{0:T(512)} %param.28) | copy-start | bytes 6136
  61.2 4.5 %copy-start.9 = (bf16[2,16,128]{2,1,0:T(8,128)(2,1)S(1)}, bf16[2,16,128]{2,1,0:T(8,128)(2,1)}, u32[]{:S(2)}) copy-start(bf16[2,16,128]{2,1,0:T(8,128)(2,1)} %get-tuple-element.32) | copy-start | bytes 24580
  61.3 4.6 %copy-start.4 = (bf16[2,128,768]{2,1,0:T(8,128)(2,1)S(1)}, bf16[2,128,768]{2,1,0:T(8,128)(2,1)}, u32[]{:S(2)}) copy-start(bf16[2,128,768]{2,1,0:T(8,128)(2,1)} %get-tuple-element.31) | copy-start | bytes 1179652
  61.3 5.7 %copy-start.1 = (bf16[1,128,768]{2,1,0:T(8,128)(2,1)S(1)}, bf16[1,128,768]{2,1,0:T(8,128)(2,1)}, u32[]{:S(2)}) copy-start(bf16[1,128,768]{2,1,0:T(8,128)(2,1)} %param.15) | copy-start | bytes 589828
  65.6 8.9 %copy-start = (bf16[32,24,768]{2,1,0:T(8,128)(2,1)}, bf16[32,24,768]{2,1,0:T(8,128)(2,1)S(1)}, u32[]{:S(2)}) copy-start(bf16[32,24,768]{2,1,0:T(8,128)(2,1)S(1)} %get-tuple-element.74) | copy-start | bytes 3538948
  74.5 2.0 copy-start.8
  74.5 2.1 copy-start.11
  74.5 2.5 %copy-start.5 = (bf16[1,128,768]{2,1,0:T(8,128)(2,1)S(1)}, bf16[1,128,768]{2,1,0:T(8,128)(2,1)}, u32[]{:S(2)}) copy-start(bf16[1,128,768]{2,1,0:T(8,128)(2,1)} %param.29) | copy-start | bytes 589828
  116.5 100.5 %collective-permute-start = (bf16[2,768,768]{2,1,0:T(8,128)(2,1)}, bf16[2,768,768]{2,1,0:T(8,128)(2,1)}, u32[]{:S(2)}, u32[]{:S(2)}) collective-permute-start(bf16[2,768,768]{2,1,0:T(8,128)(2,1)} %get-tuple-element.47), channel_id=1, source_target_pairs={{0,16},{16,0},{1,17},{17,1},{2,18},{18,2},{3,19},{19,3},{4,20},{20... | collective-permute-start | bytes 7077896 | tf_op jit(solution)/shard_map/ppermute | solution.py:580
  132.6 3.9 %copy-start.7 = (f32[16,384]{1,0:T(8,128)S(1)}, f32[16,384]{1,0:T(8,128)}, u32[]{:S(2)}) copy-start(f32[16,384]{1,0:T(8,128)} %get-tuple-element.42) | copy-start | bytes 73732
  132.7 4.6 %copy-start.2 = (f32[256,768]{1,0:T(8,128)S(1)}, f32[256,768]{1,0:T(8,128)}, u32[]{:S(2)}) copy-start(f32[256,768]{1,0:T(8,128)} %get-tuple-element.40) | copy-start | bytes 2359300
  138.0 72.7 %copy-start.3 = (f32[128,768]{1,0:T(8,128)S(1)}, f32[128,768]{1,0:T(8,128)}, u32[]{:S(2)}) copy-start(f32[128,768]{1,0:T(8,128)} %get-tuple-element.39) | copy-start | bytes 1179652
  210.6 6.3 %copy-start.6 = (bf16[2,768,768]{2,1,0:T(8,128)(2,1)S(1)}, bf16[2,768,768]{2,1,0:T(8,128)(2,1)}, u32[]{:S(2)}) copy-start(bf16[2,768,768]{2,1,0:T(8,128)(2,1)} %get-tuple-element.46) | copy-start | bytes 7077892
